TPU v7x, 32 devices: a whole 2x2x4 slice. The times are simulated.
32 devices in a mesh: dp: 2 (over x), expert: 16 (over z, y, core).
Axes of the slice: x: 2, y: 2, z: 4, core: 2. Of those that a mesh axis runs over, the one named last changes fastest.
Arguments:
- tokens: bfloat16 [2, 1024, 2048], P(None, 'expert', 'dp'), may hold values from -6 to 6
- cotangent: bfloat16 [2, 1024, 2048], P(None, 'expert', 'dp'), may hold values from -6 to 6
- routes: int32 [2, 1024, 2], P(None, 'expert'), may hold values from 0 to 15, all different within a row; in each aligned block of 64 rows (0 to 63, 64 to 127, ..., all dimensions but the last counted through in order) at most 12 rows name the same one
- gates: float32 [2, 1024, 2], P(None, 'expert'), may hold values from 0.25 to 1
- source: int32 [16], replicated, may hold values from 0 to 15, as said below
- w_gate_up: bfloat16 [16, 2048, 2, 1024], P('expert', None, None, 'dp'), may hold values from -0.125 to 0.125
- w_down: bfloat16 [16, 1024, 2048], P('expert', 'dp'), may hold values from -0.1875 to 0.1875
- moment_first: bfloat16 [16, 1024, 2048], P('expert', 'dp'), may hold values from -6 to 6
- moment_second: bfloat16 [16, 1024, 2048], P('expert', 'dp'), may hold values from 0.25 to 4
Outputs:
- layer_out: bfloat16 [2, 1024, 2048], P(None, 'expert', 'dp')
- token_grad: bfloat16 [2, 1024, 2048], P(None, 'expert', 'dp')
- update_dir: bfloat16 [16, 1024, 2048], P('expert', 'dp')
- new_first: bfloat16 [16, 1024, 2048], P('expert', 'dp')
- new_second: bfloat16 [16, 1024, 2048], P('expert', 'dp')
Inputs may be any that keep to these rules, and one draw needn't show every extreme that they name: `routes`: in each micro-batch, the 64 tokens of one index of expert name no expert more than 12 times, a bound that some block reaches. source[source[s]] = s for every slot; 8 slots take another slot's expert.
All inputs are finite; a program needn't handle non-finite values.
Results may differ from a plain program's by a relative error of at most 0.018.
Values may be sent and summed in bfloat16 or wider, within the bound.
No kernel may reach another device: no remote copies, remote signals or barrier semaphores. Data moves between devices by JAX's collectives and lax.ppermute only.
A program may use at most 128 MiB of HBM per device.

v0:
```python
import functools

import jax
import jax.numpy as jnp
from jax import lax
from jax.experimental import pallas as pl
from jax.experimental.pallas import tpu as pltpu
from jax.sharding import PartitionSpec as P

contract_first = (((0,), (0,)), ((), ()))
contract_second = (((1,), (1,)), ((), ()))
VMEM_BYTES = 32 * 1024 * 1024


def fence(*values):
    return lax.optimization_barrier(values)


def exchange(blocks):
    return lax.all_to_all(blocks, "expert", split_axis=0, concat_axis=0, tiled=True)


def reorder_kernel(order_ref, blocks_ref, out_ref):
    for place in range(out_ref.shape[0]):
        out_ref[place] = blocks_ref[order_ref[place]]


def reorder(blocks, order):
    whole = pl.BlockSpec(memory_space=pltpu.VMEM)
    return pl.pallas_call(
        reorder_kernel,
        out_shape=jax.ShapeDtypeStruct(blocks.shape, blocks.dtype),
        in_specs=[pl.BlockSpec(memory_space=pltpu.SMEM), whole],
        out_specs=whole,
        compiler_params=pltpu.CompilerParams(vmem_limit_bytes=VMEM_BYTES),
        name="reorder",
    )(order, blocks)


def gather_features(rows):
    parts = lax.axis_size("dp")
    if parts == 2:
        other = lax.ppermute(rows, "dp", ((0, 1), (1, 0)))
        first = lax.axis_index("dp") == 0
        return [jnp.where(first, rows, other), jnp.where(first, other, rows)]
    whole = lax.all_gather(rows, "dp", axis=0, tiled=False)
    return [whole[part] for part in range(parts)]


def scatter_sum(partial):
    parts = lax.axis_size("dp")
    if parts == 2:
        half = partial.shape[1] // 2
        low, high = partial[:, :half], partial[:, half:]
        first = lax.axis_index("dp") == 0
        keep, send = jnp.where(first, low, high), jnp.where(first, high, low)
        other = lax.ppermute(send, "dp", ((0, 1), (1, 0)))
        return (keep.astype(jnp.float32) + other.astype(jnp.float32)).astype(jnp.bfloat16)
    return lax.psum_scatter(partial, "dp", scatter_dimension=1, tiled=True)


def relocate_spread(arrays, source, experts):
    outputs = []
    for array in arrays:
        blocks = array.reshape(experts, array.shape[1] // experts, array.shape[2])
        outputs.append(exchange(reorder(exchange(blocks), source)).reshape(array.shape[1:]))
    return outputs


PLANES = 4
GROUP = 4
KINDS = (((0, 1), (1, 2), (2, 3)), ((0, 2), (2, 3)), ((0, 1), (1, 3)), ((0, 3),))
KIND_ROW, UP_ROW, DOWN_ROW, FINAL_ROW = 0, 4, 8, 12


def plan_kernel(where_ref, source_ref, plan_ref, ends_ref):
    plane = where_ref[0]
    member = where_ref[1]
    for index in range(PLANES):
        plan_ref[KIND_ROW + index] = 0
        plan_ref[UP_ROW + index] = GROUP
        plan_ref[DOWN_ROW + index] = GROUP
        ends_ref[index] = 0
    for slot in range(PLANES * GROUP):
        low = slot // GROUP
        other = source_ref[slot]
        high = other // GROUP
        offset = (slot % GROUP) ^ member

        @pl.when(jnp.logical_and(high == low, plane == low))
        def _():
            plan_ref[FINAL_ROW + offset] = (other % GROUP) ^ member

        @pl.when(high > low)
        def _():
            turn = jnp.int32(PLANES - 1)
            for index in reversed(range(PLANES - 1)):
                turn = jnp.where(ends_ref[index] <= low, index, turn)
            ends_ref[turn] = high
            span = high - low
            kind = jnp.where(span == 3, 4, jnp.where(span == 2, 2 + low, 1))
            plan_ref[KIND_ROW + turn] = jnp.maximum(plan_ref[KIND_ROW + turn], kind)

            @pl.when(plane == low)
            def _():
                plan_ref[UP_ROW + turn] = offset
                plan_ref[FINAL_ROW + offset] = GROUP + 2 * turn + 1

            @pl.when(plane == high)
            def _():
                there = (other % GROUP) ^ member
                plan_ref[DOWN_ROW + turn] = there
                plan_ref[FINAL_ROW + there] = GROUP + 2 * turn


def make_plan(source, plane, member):
    smem = pl.BlockSpec(memory_space=pltpu.SMEM)
    return pl.pallas_call(
        plan_kernel,
        out_shape=jax.ShapeDtypeStruct((16,), jnp.int32),
        in_specs=[smem, smem],
        out_specs=smem,
        scratch_shapes=[pltpu.SMEM((PLANES,), jnp.int32)],
        name="plan",
    )(jnp.stack([plane, member]), source)


def cut_kernel(member_ref, *refs):
    count = (len(refs) - 3) // (1 + GROUP)
    arrays, outs = refs[:count], refs[count:-3]
    staged, in_sems, out_sems = refs[-3:]
    rows = outs[0].shape[0]
    loads, stores = [], []
    for which, array in enumerate(arrays):
        for offset in (2, 3, 1, 0):
            begin = pl.multiple_of((member_ref[0] ^ offset) * rows, rows)
            place = which * GROUP + offset
            loads.append(
                pltpu.make_async_copy(
                    array.at[pl.ds(begin, rows)], staged.at[place], in_sems.at[place]
                )
            )
            stores.append(
                pltpu.make_async_copy(staged.at[place], outs[place], out_sems.at[place])
            )
    for load in loads:
        load.start()
    for load, store in zip(loads, stores):
        load.wait()
        store.start()
    for store in stores:
        store.wait()


def cut(arrays, member):
    rows, width = arrays[0].shape
    anywhere = pl.BlockSpec(memory_space=pl.ANY)
    piece = (rows // GROUP, width)
    amount = GROUP * len(arrays)
    pieces = pl.pallas_call(
        cut_kernel,
        out_shape=[jax.ShapeDtypeStruct(piece, arrays[0].dtype)] * amount,
        in_specs=[pl.BlockSpec(memory_space=pltpu.SMEM)] + [anywhere] * len(arrays),
        out_specs=[anywhere] * amount,
        scratch_shapes=[
            pltpu.VMEM((amount, *piece), arrays[0].dtype),
            pltpu.SemaphoreType.DMA((amount,)),
            pltpu.SemaphoreType.DMA((amount,)),
        ],
        compiler_params=pltpu.CompilerParams(vmem_limit_bytes=VMEM_BYTES),
        name="cut",
    )(member[None], *arrays)
    return [list(pieces[at : at + GROUP]) for at in range(0, amount, GROUP)]


def choose_kernel(count, choice_ref, *refs):
    options, outs = refs[:count], refs[count:-3]
    staged, in_sems, out_sems = refs[-3:]
    for place in range(len(outs)):
        for index, option in enumerate(options):

            @pl.when(choice_ref[place] == index)
            def _():
                pltpu.make_async_copy(option, staged.at[place], in_sems.at[place]).start()

    for place, out in enumerate(outs):

        @pl.when(choice_ref[place] < count)
        def _():
            pltpu.make_async_copy(options[0], staged.at[place], in_sems.at[place]).wait()
            pltpu.make_async_copy(staged.at[place], out, out_sems.at[place]).start()

    for place, out in enumerate(outs):

        @pl.when(choice_ref[place] < count)
        def _():
            pltpu.make_async_copy(staged.at[place], out, out_sems.at[place]).wait()


def choose(choice, options):
    anywhere = pl.BlockSpec(memory_space=pl.ANY)
    shape, dtype = options[0].shape, options[0].dtype
    amount = choice.shape[0]
    return pl.pallas_call(
        functools.partial(choose_kernel, len(options)),
        out_shape=[jax.ShapeDtypeStruct(shape, dtype)] * amount,
        in_specs=[pl.BlockSpec(memory_space=pltpu.SMEM)] + [anywhere] * len(options),
        out_specs=[anywhere] * amount,
        scratch_shapes=[
            pltpu.VMEM((amount, *shape), dtype),
            pltpu.SemaphoreType.DMA((amount,)),
            pltpu.SemaphoreType.DMA((amount,)),
        ],
        compiler_params=pltpu.CompilerParams(vmem_limit_bytes=VMEM_BYTES),
        name="choose",
    )(choice, *options)


def within_plane(offset):
    return [(index, index ^ offset) for index in range(PLANES * GROUP)]


def between_planes(moves):
    return [(GROUP * a + index, GROUP * b + index) for a, b in moves for index in range(GROUP)]


def swap_round(moves):
    def run(up, down):
        return (
            lax.ppermute(up, "expert", between_planes(moves)),
            lax.ppermute(down, "expert", between_planes([(b, a) for a, b in moves])),
        )

    return run


def hand_over(pieces):
    return list(pieces[:1]) + [
        lax.ppermute(pieces[offset], "expert", within_plane(offset)) for offset in range(1, GROUP)
    ]


def swap_pieces(turn, plan, ways):
    return list(
        lax.switch(
            plan[KIND_ROW + turn],
            [lambda up, down: (up, down)] + [swap_round(moves) for moves in KINDS],
            ways[turn],
            ways[PLANES + turn],
        )
    )


def join_quarters(own):
    member = lax.axis_index("expert") % GROUP
    for bit in (1, 2):
        swap = (member & bit) != 0
        own = [jnp.where(swap, own[offset ^ bit], own[offset]) for offset in range(GROUP)]
    return jnp.concatenate(own, axis=0)


def per_device(
    tokens, cotangent, routes, gates, source, w_gate_up, w_down, moment_first, moment_second
):
    experts = lax.axis_size("expert")
    micro_count, token_count, part_width = tokens.shape
    model_width = w_gate_up.shape[1]
    hidden_part = w_gate_up.shape[3]
    top_count = routes.shape[2]
    capacity = max(2, 3 * token_count * top_count // (2 * experts))
    per_expert = micro_count * capacity
    slots = experts * per_expert
    all_tokens = micro_count * token_count
    swaps = experts == PLANES * GROUP

    pairs = token_count * top_count
    chosen = routes.reshape(micro_count, pairs)
    same = chosen[:, :, None] == chosen[:, None, :]
    order = jnp.arange(pairs, dtype=jnp.int32)
    earlier = order[None, :] < order[:, None]
    position = jnp.sum((same & earlier).astype(jnp.int32), axis=2)
    micro_ids = jnp.arange(micro_count, dtype=jnp.int32)[:, None]
    place = (chosen * per_expert + micro_ids * capacity + position).reshape(all_tokens, top_count)
    slot_ids = jnp.arange(slots, dtype=jnp.int32)
    flat_gates = gates.reshape(all_tokens, top_count)
    matches = [place[:, k][:, None] == slot_ids for k in range(top_count)]
    picks = [match.astype(jnp.bfloat16) for match in matches]
    plain = sum(picks[1:], picks[0])
    slot_gate = sum(
        jnp.sum(jnp.where(matches[k], flat_gates[:, k : k + 1], 0.0), axis=0)
        for k in range(top_count)
    )

    row_tokens = lax.dot_general(
        plain,
        tokens.reshape(all_tokens, part_width),
        contract_first,
        preferred_element_type=jnp.float32,
    ).astype(jnp.bfloat16)
    if swaps:
        index = lax.axis_index("expert")
        plane, member = index // GROUP, index % GROUP
        plan = make_plan(source, plane, member)
        row_tokens, (pieces_a, pieces_b) = fence(
            row_tokens, cut((moment_first[0], moment_second[0]), member)
        )
        held_a = hand_over(pieces_a)
    here_tokens = exchange(row_tokens.reshape(experts, per_expert, part_width))
    row_grads = (
        lax.dot_general(
            plain,
            cotangent.reshape(all_tokens, part_width),
            contract_first,
            preferred_element_type=jnp.float32,
        )
        * slot_gate[:, None]
    ).astype(jnp.bfloat16)
    gate_up = w_gate_up.reshape(model_width, 2 * hidden_part)
    down = w_down.reshape(hidden_part, model_width)

    if swaps:
        here_tokens, row_grads, gate_up, held_a, pieces_b, plan = fence(
            here_tokens, row_grads, gate_up, held_a, pieces_b, plan
        )
        held_b = hand_over(pieces_b)
        ways_a = choose(plan[UP_ROW:FINAL_ROW], held_a)
        arrived_a = swap_pieces(0, plan, ways_a) + swap_pieces(1, plan, ways_a)
    grad_blocks = row_grads.reshape(experts, per_expert, part_width)
    here_grads = exchange(grad_blocks)
    expert_in = jnp.concatenate(gather_features(here_tokens.reshape(slots, part_width)), axis=1)
    if swaps:
        expert_in, here_grads, arrived_a, held_b = fence(
            expert_in, here_grads, arrived_a, held_b
        )
    both = jnp.dot(expert_in, gate_up, preferred_element_type=jnp.float32)
    gate_pre = both[:, :hidden_part]
    up_pre = both[:, hidden_part:]
    gate_sig = jax.nn.sigmoid(gate_pre)
    hidden = (gate_pre * gate_sig * up_pre).astype(jnp.bfloat16)
    partial_out = jnp.dot(hidden, down, preferred_element_type=jnp.float32).astype(jnp.bfloat16)

    if swaps:
        hidden, partial_out, ways_a, held_b = fence(hidden, partial_out, ways_a, held_b)
        arrived_a += swap_pieces(2, plan, ways_a) + swap_pieces(3, plan, ways_a)
        ways_b = choose(plan[UP_ROW:FINAL_ROW], held_b)
        arrived_b = swap_pieces(0, plan, ways_b)
    summed_out = scatter_sum(partial_out)

    if swaps:
        summed_out, here_grads, arrived_a, arrived_b, ways_b = fence(
            summed_out, here_grads, arrived_a, arrived_b, ways_b
        )
        own_a = hand_over(choose(plan[FINAL_ROW:], [*held_a, *arrived_a]))
        arrived_b += swap_pieces(1, plan, ways_b)
    back = exchange(
        jnp.concatenate([summed_out, hidden], axis=1).reshape(experts, per_expert, -1)
    )
    grad_in = jnp.concatenate(gather_features(here_grads.reshape(slots, part_width)), axis=1)
    hidden_grad = lax.dot_general(
        grad_in, down, contract_second, preferred_element_type=jnp.float32
    )
    gate_grad = hidden_grad * up_pre * gate_sig * (1.0 + gate_pre * (1.0 - gate_sig))
    up_grad = hidden_grad * gate_pre * gate_sig
    both_grad = jnp.concatenate([gate_grad, up_grad], axis=1).astype(jnp.bfloat16)
    partial_in = lax.dot_general(
        both_grad, gate_up, contract_second, preferred_element_type=jnp.float32
    ).astype(jnp.bfloat16)
    to_move = reorder(jnp.concatenate([back[:, :, part_width:], grad_blocks], axis=2), source)

    if swaps:
        to_move, partial_in, own_a, arrived_b, ways_b = fence(
            to_move, partial_in, own_a, arrived_b, ways_b
        )
        arrived_b += swap_pieces(2, plan, ways_b) + swap_pieces(3, plan, ways_b)
        ready_b = choose(plan[FINAL_ROW:], [*held_b, *arrived_b])
    there = exchange(to_move).reshape(slots, hidden_part + part_width)
    summed_in = scatter_sum(partial_in)
    back_out = back[:, :, :part_width].reshape(slots, part_width)
    layer_out = sum(
        flat_gates[:, k : k + 1] * jnp.dot(picks[k], back_out, preferred_element_type=jnp.float32)
        for k in range(top_count)
    ).astype(jnp.bfloat16)

    if swaps:
        there, summed_in, ready_b, layer_out = fence(there, summed_in, ready_b, layer_out)
        own_b = hand_over(ready_b)
    back_in = exchange(summed_in.reshape(experts, per_expert, part_width))
    token_grad = jnp.dot(
        plain, back_in.reshape(slots, part_width), preferred_element_type=jnp.float32
    )

    there_hidden = there[:, :hidden_part]
    there_grads = jnp.concatenate(gather_features(there[:, hidden_part:]), axis=1)
    if swaps:
        old_first, old_second = join_quarters(own_a), join_quarters(own_b)
    else:
        old_first, old_second = relocate_spread((moment_first, moment_second), source, experts)
    down_grad = lax.dot_general(
        there_hidden, there_grads, contract_first, preferred_element_type=jnp.float32
    )
    first = 0.9 * old_first.astype(jnp.float32) + 0.1 * down_grad
    second = 0.999 * old_second.astype(jnp.float32) + 0.001 * down_grad * down_grad
    update = first / (jnp.sqrt(second) + 1e-08)
    shape = moment_first.shape
    return (
        layer_out.reshape(tokens.shape),
        token_grad.astype(jnp.bfloat16).reshape(tokens.shape),
        update.astype(jnp.bfloat16).reshape(shape),
        first.astype(jnp.bfloat16).reshape(shape),
        second.astype(jnp.bfloat16).reshape(shape),
    )


def solution(mesh):
    placed = (
        P(None, "expert", "dp"),
        P(None, "expert", "dp"),
        P(None, "expert", None),
        P(None, "expert", None),
        P(),
        P("expert", None, None, "dp"),
        P("expert", "dp", None),
        P("expert", "dp", None),
        P("expert", "dp", None),
    )
    return jax.shard_map(
        per_device,
        mesh=mesh,
        in_specs=placed,
        out_specs=(
            P(None, "expert", "dp"),
            P(None, "expert", "dp"),
            P("expert", "dp", None),
            P("expert", "dp", None),
            P("expert", "dp", None),
        ),
        check_vma=False,
    )
```

profile of v0, /device:TPU:8, one launch (start us, length us, event | category | flops | bytes accessed | tf_op | source)
XLA Modules:
  0.0 293.0 jit_solution(5990110337322841400)
XLA Ops:
  3.1 2.3 convolution_convert_fusion.2
  5.4 1.6 copy-done.11
  7.0 1.6 copy-done.12
  15.0 6.3 %all-to-all-start = ((bf16[16,24,1024]{2,1,0:T(8,128)(2,1)}), bf16[16,24,1024]{2,1,0:T(8,128)(2,1)}, u32[]{:S(2)}, u32[]{:S(2)}) async-start(bf16[16,24,1024]{2,1,0:T(8,128)(2,1)} %bitcast.72), calls=%async_computation | async-start | bytes 1572864 | tf_op jit(solution)/shard_map/all_to_all | solution.py:20
  21.4 1.5 collective-permute-start.65
  23.2 5.5 %copy.22 = bf16[256,8,2,512]{3,1,2,0:T(8,128)(2,1)} copy(bf16[256,8,2,512]{3,2,1,0:T(2,128)(2,1)} %bitcast.69) | data formatting | bytes 8388608
  29.3 1.5 plan.1
  31.3 1.4 multiply_convert_fusion
  32.7 11.4 %collective-permute-done.65.refs_2_ = bf16[128,2048]{1,0:T(8,128)(2,1)} collective-permute-done((bf16[128,2048]{1,0:T(8,128)(2,1)}, bf16[128,2048]{1,0:T(8,128)(2,1)}, u32[]{:S(2)}, u32[]{:S(2)}) %collective-permute-start.65) | collective-permute-done | bytes 524320 | tf_op jit(solution)/shard_map/ppermute | solution.py:239
  44.2 10.3 %collective-permute-done.66.refs_3_ = bf16[128,2048]{1,0:T(8,128)(2,1)} collective-permute-done((bf16[128,2048]{1,0:T(8,128)(2,1)}, bf16[128,2048]{1,0:T(8,128)(2,1)}, u32[]{:S(2)}, u32[]{:S(2)}) %collective-permute-start.66) | collective-permute-done | bytes 524320 | tf_op jit(solution)/shard_map/ppermute | solution.py:239
  54.5 5.1 %all-to-all-start.1 = ((bf16[16,24,1024]{2,1,0:T(8,128)(2,1)}), bf16[16,24,1024]{2,1,0:T(8,128)(2,1)}, u32[]{:S(2)}, u32[]{:S(2)}) async-start(bf16[16,24,1024]{2,1,0:T(8,128)(2,1)} %bitcast.64), calls=%async_computation.1 | async-start | bytes 1572864 | tf_op jit(solution)/shard_map/all_to_all | solution.py:20
  59.6 1.5 collective-permute-start.67
  63.2 1.5 collective-permute-start.69
  66.8 2.6 choose.4
  69.4 21.1 %conditional.9 = (bf16[128,2048]{1,0:T(8,128)(2,1)}, bf16[128,2048]{1,0:T(8,128)(2,1)}) conditional(s32[]{:T(128)} %bitcast.14, (bf16[128,2048]{1,0:T(8,128)(2,1)S(1)}, bf16[128,2048]{1,0:T(8,128)(2,1)S(1)}) %tuple.171, (bf16[128,2048]{1,0:T(8,128)(2,1)S(1)}, bf16[128,2048]{1,0:T(8,128)(2,1)S(1)}) %tuple.171, ...), branch_computations={%region_8.9_spmd, %region_9.10_spmd, %region_10.11_spmd, %region_1... | conditional | bytes 4194400 | solution.py:245
  69.4 2.7 collective-permute-start.8
  72.2 3.9 %collective-permute-start.9 = (bf16[128,2048]{1,0:T(8,128)(2,1)S(1)}, bf16[128,2048]{1,0:T(8,128)(2,1)}, u32[]{:S(2)}, u32[]{:S(2)}) collective-permute-start(bf16[128,2048]{1,0:T(8,128)(2,1)S(1)} %get-tuple-element.169), channel_id=1, source_target_pairs={{4,0},{5,1},{6,2},{7,3},{8,4},{9,5},{10,6},{11,7},{12,8},{13,9},{1... | collective-permute-start | bytes 1572872 | tf_op jit(solution)/shard_map/cond/branch_1_fun/ppermute | solution.py:231
  76.1 12.4 %collective-permute-done.8 = bf16[128,2048]{1,0:T(8,128)(2,1)} collective-permute-done((bf16[128,2048]{1,0:T(8,128)(2,1)S(1)}, bf16[128,2048]{1,0:T(8,128)(2,1)}, u32[]{:S(2)}, u32[]{:S(2)}) %collective-permute-start.8) | collective-permute-done | bytes 524320 | tf_op jit(solution)/shard_map/cond/branch_1_fun/ppermute | solution.py:230
  88.5 2.0 collective-permute-done.9
  90.5 17.9 %conditional.8 = (bf16[128,2048]{1,0:T(8,128)(2,1)}, bf16[128,2048]{1,0:T(8,128)(2,1)}) conditional(s32[]{:T(128)} %bitcast.13, (bf16[128,2048]{1,0:T(8,128)(2,1)}, bf16[128,2048]{1,0:T(8,128)(2,1)}) %tuple.170, (bf16[128,2048]{1,0:T(8,128)(2,1)}, bf16[128,2048]{1,0:T(8,128)(2,1)}) %tuple.170, ...), branch_computations={%region_3.4_spmd, %region_4.5_spmd, %region_5.6_spmd, %region_6.7_... | conditional | bytes 4194400 | solution.py:245
  90.5 2.5 collective-permute-start
  93.0 4.1 %collective-permute-start.1 = (bf16[128,2048]{1,0:T(8,128)(2,1)}, bf16[128,2048]{1,0:T(8,128)(2,1)}, u32[]{:S(2)}, u32[]{:S(2)}) collective-permute-start(bf16[128,2048]{1,0:T(8,128)(2,1)} %get-tuple-element.161), channel_id=1, source_target_pairs={{4,0},{5,1},{6,2},{7,3},{8,4},{9,5},{10,6},{11,7},{12,8},{13,9},{1... | collective-permute-start | bytes 1572872 | tf_op jit(solution)/shard_map/cond/branch_1_fun/ppermute | solution.py:231
  97.2 9.0 %collective-permute-done = bf16[128,2048]{1,0:T(8,128)(2,1)} collective-permute-done((bf16[128,2048]{1,0:T(8,128)(2,1)}, bf16[128,2048]{1,0:T(8,128)(2,1)}, u32[]{:S(2)}, u32[]{:S(2)}) %collective-permute-start) | collective-permute-done | bytes 524320 | tf_op jit(solution)/shard_map/cond/branch_1_fun/ppermute | solution.py:230
  106.2 2.2 collective-permute-done.1
  108.4 1.5 broadcast_select_fusion.7
  109.9 1.2 pad_maximum_fusion.2
  111.1 11.7 %collective-permute-done.70.refs_3_ = bf16[128,2048]{1,0:T(8,128)(2,1)S(1)} collective-permute-done((bf16[128,2048]{1,0:T(8,128)(2,1)}, bf16[128,2048]{1,0:T(8,128)(2,1)S(1)}, u32[]{:S(2)}, u32[]{:S(2)}) %collective-permute-start.70) | collective-permute-done | bytes 524320 | tf_op jit(solution)/shard_map/ppermute | solution.py:239
  123.6 4.4 %fusion.44 = f32[384,1024]{1,0:T(8,128)S(1)} fusion(bf16[384,2048]{1,0:T(8,128)(2,1)} %pad_maximum_fusion.2, bf16[2048,1024]{1,0:T(8,128)(2,1)} %bitcast.70), kind=kOutput, calls=%fused_computation.96 | convolution fusion | flops 1610612736 | bytes 7340032 | tf_op jit(solution)/shard_map/dot_general | solution.py:335
  131.5 1.5 collective-permute-start.71
  134.2 1.9 choose.5
  136.2 17.5 %conditional.12 = (bf16[128,2048]{1,0:T(8,128)(2,1)}, bf16[128,2048]{1,0:T(8,128)(2,1)}) conditional(s32[]{:T(128)} %bitcast.13, (bf16[128,2048]{1,0:T(8,128)(2,1)S(1)}, bf16[128,2048]{1,0:T(8,128)(2,1)S(1)}) %tuple.176, (bf16[128,2048]{1,0:T(8,128)(2,1)S(1)}, bf16[128,2048]{1,0:T(8,128)(2,1)S(1)}) %tuple.176, ...), branch_computations={%region_23.24_spmd, %region_24.25_spmd, %region_25.26_spmd, %regio... | conditional | bytes 4194400 | solution.py:245
  136.2 2.9 collective-permute-start.32
  139.1 3.8 %collective-permute-start.33 = (bf16[128,2048]{1,0:T(8,128)(2,1)S(1)}, bf16[128,2048]{1,0:T(8,128)(2,1)}, u32[]{:S(2)}, u32[]{:S(2)}) collective-permute-start(bf16[128,2048]{1,0:T(8,128)(2,1)S(1)} %get-tuple-element.193), channel_id=1, source_target_pairs={{4,0},{5,1},{6,2},{7,3},{8,4},{9,5},{10,6},{11,7},{12,8},{13,9},{1... | collective-permute-start | bytes 1572872 | tf_op jit(solution)/shard_map/cond/branch_1_fun/ppermute | solution.py:231
  142.9 8.8 %collective-permute-done.32 = bf16[128,2048]{1,0:T(8,128)(2,1)} collective-permute-done((bf16[128,2048]{1,0:T(8,128)(2,1)S(1)}, bf16[128,2048]{1,0:T(8,128)(2,1)}, u32[]{:S(2)}, u32[]{:S(2)}) %collective-permute-start.32) | collective-permute-done | bytes 524320 | tf_op jit(solution)/shard_map/cond/branch_1_fun/ppermute | solution.py:230
  151.6 2.0 collective-permute-done.33
  153.7 2.0 add_convert_fusion.1
  156.8 6.6 %all-to-all-start.2 = ((bf16[16,24,1536]{2,1,0:T(8,128)(2,1)}), bf16[16,24,1536]{2,1,0:T(8,128)(2,1)}, u32[]{:S(2)}, u32[]{:S(2)}) async-start(bf16[16,24,1536]{2,1,0:T(8,128)(2,1)} %bitcast.68), calls=%async_computation.2 | async-start | bytes 2359296 | tf_op jit(solution)/shard_map/all_to_all | solution.py:20
  166.1 2.8 choose.6
  170.5 1.4 collective-permute-start.74
  171.9 30.9 %conditional.13 = (bf16[128,2048]{1,0:T(8,128)(2,1)}, bf16[128,2048]{1,0:T(8,128)(2,1)}) conditional(s32[]{:T(128)} %bitcast.14, (bf16[128,2048]{1,0:T(8,128)(2,1)S(1)}, bf16[128,2048]{1,0:T(8,128)(2,1)S(1)}) %tuple.282, (bf16[128,2048]{1,0:T(8,128)(2,1)S(1)}, bf16[128,2048]{1,0:T(8,128)(2,1)S(1)}) %tuple.283, ...), branch_computations={%region_28.29_spmd, %region_29.30_spmd, %region_30.31_spmd, %regio... | conditional | bytes 4194400 | solution.py:245
  171.9 3.4 %collective-permute-start.40 = (bf16[128,2048]{1,0:T(8,128)(2,1)S(1)}, bf16[128,2048]{1,0:T(8,128)(2,1)}, u32[]{:S(2)}, u32[]{:S(2)}) collective-permute-start(bf16[128,2048]{1,0:T(8,128)(2,1)S(1)} %get-tuple-element.200), channel_id=1, source_target_pairs={{0,4},{1,5},{2,6},{3,7},{4,8},{5,9},{6,10},{7,11},{8,12},{9,13},{1... | collective-permute-start | bytes 1572872 | tf_op jit(solution)/shard_map/cond/branch_1_fun/ppermute | solution.py:230
  175.3 3.2 %collective-permute-start.41 = (bf16[128,2048]{1,0:T(8,128)(2,1)S(1)}, bf16[128,2048]{1,0:T(8,128)(2,1)}, u32[]{:S(2)}, u32[]{:S(2)}) collective-permute-start(bf16[128,2048]{1,0:T(8,128)(2,1)S(1)} %get-tuple-element.201), channel_id=1, source_target_pairs={{4,0},{5,1},{6,2},{7,3},{8,4},{9,5},{10,6},{11,7},{12,8},{13,9},{1... | collective-permute-start | bytes 1572872 | tf_op jit(solution)/shard_map/cond/branch_1_fun/ppermute | solution.py:231
  178.5 22.2 %collective-permute-done.40 = bf16[128,2048]{1,0:T(8,128)(2,1)} collective-permute-done((bf16[128,2048]{1,0:T(8,128)(2,1)S(1)}, bf16[128,2048]{1,0:T(8,128)(2,1)}, u32[]{:S(2)}, u32[]{:S(2)}) %collective-permute-start.40) | collective-permute-done | bytes 524320 | tf_op jit(solution)/shard_map/cond/branch_1_fun/ppermute | solution.py:230
  200.8 2.1 collective-permute-done.41
  203.6 1.5 broadcast_select_fusion.4
  205.1 1.3 multiply_convert_fusion.2
  207.3 3.0 %convolution_convert_fusion = bf16[384,2048]{1,0:T(8,128)(2,1)} fusion(bf16[2048,1024]{1,0:T(8,128)(2,1)S(1)} %bitcast.71, bf16[384,512]{1,0:T(8,128)(2,1)S(1)} %get-tuple-element.489, bf16[384,512]{1,0:T(8,128)(2,1)S(1)} %get-tuple-element.488), kind=kOutput, calls=%fused_computation.4 | convolution fusion | flops 1612972032 | bytes 6553600 | tf_op jit(solution)/shard_map/dot_general | solution.py:365
  211.4 1.6 reorder.1
  213.0 4.3 %collective-permute-done.75 = bf16[128,2048]{1,0:T(8,128)(2,1)} collective-permute-done((bf16[128,2048]{1,0:T(8,128)(2,1)}, bf16[128,2048]{1,0:T(8,128)(2,1)}, u32[]{:S(2)}, u32[]{:S(2)}) %collective-permute-start.75) | collective-permute-done | bytes 524320 | tf_op jit(solution)/shard_map/ppermute | solution.py:239
  217.3 4.4 %all-to-all-start.3 = ((bf16[16,24,1536]{2,1,0:T(8,128)(2,1)}), bf16[16,24,1536]{2,1,0:T(8,128)(2,1)}, u32[]{:S(2)}, u32[]{:S(2)}) async-start(bf16[16,24,1536]{2,1,0:T(8,128)(2,1)} %reorder.1), calls=%async_computation.3 | async-start | bytes 2359296 | tf_op jit(solution)/shard_map/all_to_all | solution.py:20
  226.0 1.9 choose.7
  228.0 1.6 slice.91
  231.0 11.6 %collective-permute-done.76 = bf16[384,1024]{1,0:T(8,128)(2,1)} collective-permute-done((bf16[384,1024]{1,0:T(8,128)(2,1)}, bf16[384,1024]{1,0:T(8,128)(2,1)}, u32[]{:S(2)}, u32[]{:S(2)}) %collective-permute-start.76) | collective-permute-done | bytes 786464 | tf_op jit(solution)/shard_map/ppermute | solution.py:57
  242.5 2.6 add_convert_fusion
  245.1 3.5 %all-to-all-done.3 = bf16[16,24,1536]{2,1,0:T(8,128)(2,1)} async-done(((bf16[16,24,1536]{2,1,0:T(8,128)(2,1)}), bf16[16,24,1536]{2,1,0:T(8,128)(2,1)}, u32[]{:S(2)}, u32[]{:S(2)}) %all-to-all-start.3) | async-done | bytes 1179680 | tf_op jit(solution)/shard_map/all_to_all | solution.py:20
  248.6 2.0 collective-permute-start.78
  251.0 2.1 slice.87
  253.7 3.0 %broadcast_select_fusion.23 = (bf16[128,2048]{1,0:T(8,128)(2,1)}, bf16[128,2048]{1,0:T(8,128)(2,1)}, bf16[128,2048]{1,0:T(8,128)(2,1)}, bf16[128,2048]{1,0:T(8,128)(2,1)}) fusion(pred[]{:T(512)S(6)} %ne.26, bf16[128,2048]{1,0:T(8,128)(2,1)} %collective-permute-done.75, bf16[128,2048]{1,0:T(8,128)(2,1)} %collective-permute-done.74, pred[]{:T(512)S(6)} %ne.27, ...), kind=kLoop, calls=%fused_computation.65 | loop fusion | flops 2097152 | bytes 4194306 | tf_op jit(solution)/shard_map/jit(_where)/select_n | solution.py:258
  256.6 5.2 %all-to-all-start.4 = ((bf16[16,24,1024]{2,1,0:T(8,128)(2,1)}), bf16[16,24,1024]{2,1,0:T(8,128)(2,1)}, u32[]{:S(2)}, u32[]{:S(2)}) async-start(bf16[16,24,1024]{2,1,0:T(8,128)(2,1)} %bitcast.73), calls=%async_computation.4 | async-start | bytes 1572864 | tf_op jit(solution)/shard_map/all_to_all | solution.py:20
  262.9 17.9 %collective-permute-done.79 = bf16[128,2048]{1,0:T(8,128)(2,1)} collective-permute-done((bf16[128,2048]{1,0:T(8,128)(2,1)S(1)}, bf16[128,2048]{1,0:T(8,128)(2,1)}, u32[]{:S(2)}, u32[]{:S(2)}) %collective-permute-start.79) | collective-permute-done | bytes 524320 | tf_op jit(solution)/shard_map/ppermute | solution.py:239
  280.8 1.4 broadcast_select_fusion.19
  282.3 1.6 broadcast_select_fusion.1
  284.2 6.6 %fusion.3 = (bf16[1,512,2048]{2,1,0:T(8,128)(2,1)}, bf16[1,512,2048]{2,1,0:T(8,128)(2,1)}, bf16[1,512,2048]{2,1,0:T(8,128)(2,1)}) fusion(bf16[128,2048]{1,0:T(8,128)(2,1)S(1)} %get-tuple-element.497, bf16[128,2048]{1,0:T(8,128)(2,1)S(1)} %get-tuple-element.496, bf16[128,2048]{1,0:T(8,128)(2,1)S(1)} %get-tuple-element.495, ...), kind=kOutput, calls=%fused_computation.8 | convolution fusion | flops 837812224 | bytes 12451840 | tf_op jit(solution)/shard_map/dot_general | solution.py:398
  290.8 2.2 convolution_convert_fusion.3
  (167 shorter events, 33.5 us)
Async XLA Ops:
  0.6 127.7 %copy-start = (bf16[1,512,2048]{2,1,0:T(8,128)(2,1)S(1)}, bf16[1,512,2048]{2,1,0:T(8,128)(2,1)}, u32[]{:S(2)}) copy-start(bf16[1,512,2048]{2,1,0:T(8,128)(2,1)} %param.55) | copy-start | bytes 6291460
  5.4 1.6 copy-start.11
  7.0 1.6 copy-start.12
  8.6 14.5 %copy-start.52 = (f32[2,64,2]{1,2,0:T(2,128)S(1)}, f32[2,64,2]{1,2,0:T(2,128)}, u32[]{:S(2)}) copy-start(f32[2,64,2]{1,2,0:T(2,128)} %param.52) | copy-start | bytes 3076
  15.0 39.5 %all-to-all-start = ((bf16[16,24,1024]{2,1,0:T(8,128)(2,1)}), bf16[16,24,1024]{2,1,0:T(8,128)(2,1)}, u32[]{:S(2)}, u32[]{:S(2)}) async-start(bf16[16,24,1024]{2,1,0:T(8,128)(2,1)} %bitcast.72), calls=%async_computation | async-start | bytes 1572864 | tf_op jit(solution)/shard_map/all_to_all | solution.py:20
  21.3 11.5 %collective-permute-start.64 = (bf16[128,2048]{1,0:T(8,128)(2,1)}, bf16[128,2048]{1,0:T(8,128)(2,1)S(1)}, u32[]{:S(2)}, u32[]{:S(2)}) collective-permute-start(bf16[128,2048]{1,0:T(8,128)(2,1)} %copy-done.26), channel_id=1, source_target_pairs={{0,1},{1,0},{2,3},{3,2},{4,5},{5,4},{6,7},{7,6},{8,9},{9,8},{10,11... | collective-permute-start | bytes 1572872 | tf_op jit(solution)/shard_map/ppermute | solution.py:239
  21.4 22.8 %collective-permute-start.65 = (bf16[128,2048]{1,0:T(8,128)(2,1)}, bf16[128,2048]{1,0:T(8,128)(2,1)}, u32[]{:S(2)}, u32[]{:S(2)}) collective-permute-start(bf16[128,2048]{1,0:T(8,128)(2,1)} %copy-done.23), channel_id=1, source_target_pairs={{0,2},{1,3},{2,0},{3,1},{4,6},{5,7},{6,4},{7,5},{8,10},{9,11},{10,... | collective-permute-start | bytes 1572872 | tf_op jit(solution)/shard_map/ppermute | solution.py:239
  22.9 31.6 %collective-permute-start.66 = (bf16[128,2048]{1,0:T(8,128)(2,1)}, bf16[128,2048]{1,0:T(8,128)(2,1)}, u32[]{:S(2)}, u32[]{:S(2)}) collective-permute-start(bf16[128,2048]{1,0:T(8,128)(2,1)} %copy-done.20), channel_id=1, source_target_pairs={{0,3},{1,2},{2,1},{3,0},{4,7},{5,6},{6,5},{7,4},{8,11},{9,10},{10,... | collective-permute-start | bytes 1572872 | tf_op jit(solution)/shard_map/ppermute | solution.py:239
  23.2 8.1 %copy-start.46 = (bf16[2,64,1024]{2,1,0:T(8,128)(2,1)S(1)}, bf16[2,64,1024]{2,1,0:T(8,128)(2,1)}, u32[]{:S(2)}) copy-start(bf16[2,64,1024]{2,1,0:T(8,128)(2,1)} %param.50) | copy-start | bytes 786436
  30.8 30.3 %copy-start.47 = (s32[16]{0:T(128)S(1)}, s32[16]{0:T(128)}, u32[]{:S(2)}) copy-start(s32[16]{0:T(128)} %plan.1) | copy-start | bytes 196
  30.8 38.6 %copy-start.50 = (f32[128]{0:T(128)}, f32[128]{0:T(128)S(1)}, u32[]{:S(2)}) copy-start(f32[128]{0:T(128)S(1)} %get-tuple-element.505) | copy-start | bytes 1540
  32.7 29.7 %copy-start.8 = (bf16[128,2048]{1,0:T(8,128)(2,1)}, bf16[128,2048]{1,0:T(8,128)(2,1)S(1)}, u32[]{:S(2)}) copy-start(bf16[128,2048]{1,0:T(8,128)(2,1)S(1)} %collective-permute-done.64.refs_1_) | copy-start | bytes 1572868
  54.5 69.2 %all-to-all-start.1 = ((bf16[16,24,1024]{2,1,0:T(8,128)(2,1)}), bf16[16,24,1024]{2,1,0:T(8,128)(2,1)}, u32[]{:S(2)}, u32[]{:S(2)}) async-start(bf16[16,24,1024]{2,1,0:T(8,128)(2,1)} %bitcast.64), calls=%async_computation.1 | async-start | bytes 1572864 | tf_op jit(solution)/shard_map/all_to_all | solution.py:20
  59.6 48.8 %collective-permute-start.67 = (bf16[384,1024]{1,0:T(8,128)(2,1)}, bf16[384,1024]{1,0:T(8,128)(2,1)}, u32[]{:S(2)}, u32[]{:S(2)}) collective-permute-start(bf16[384,1024]{1,0:T(8,128)(2,1)} %bitcast.11), channel_id=1, source_target_pairs={{0,16},{16,0},{1,17},{17,1},{2,18},{18,2},{3,19},{19,3},{4,20},{20... | collective-permute-start | bytes 2359304 | tf_op jit(solution)/shard_map/ppermute | solution.py:43
  63.1 48.1 %collective-permute-start.68 = (bf16[128,2048]{1,0:T(8,128)(2,1)}, bf16[128,2048]{1,0:T(8,128)(2,1)S(1)}, u32[]{:S(2)}, u32[]{:S(2)}) collective-permute-start(bf16[128,2048]{1,0:T(8,128)(2,1)} %copy-done.18), channel_id=1, source_target_pairs={{0,1},{1,0},{2,3},{3,2},{4,5},{5,4},{6,7},{7,6},{8,9},{9,8},{10,11... | collective-permute-start | bytes 1572872 | tf_op jit(solution)/shard_map/ppermute | solution.py:239
  63.2 48.0 %collective-permute-start.69 = (bf16[128,2048]{1,0:T(8,128)(2,1)}, bf16[128,2048]{1,0:T(8,128)(2,1)}, u32[]{:S(2)}, u32[]{:S(2)}) collective-permute-start(bf16[128,2048]{1,0:T(8,128)(2,1)} %copy-done.17), channel_id=1, source_target_pairs={{0,2},{1,3},{2,0},{3,1},{4,6},{5,7},{6,4},{7,5},{8,10},{9,11},{10,... | collective-permute-start | bytes 1572872 | tf_op jit(solution)/shard_map/ppermute | solution.py:239
  69.4 19.1 %collective-permute-start.8 = (bf16[128,2048]{1,0:T(8,128)(2,1)S(1)}, bf16[128,2048]{1,0:T(8,128)(2,1)}, u32[]{:S(2)}, u32[]{:S(2)}) collective-permute-start(bf16[128,2048]{1,0:T(8,128)(2,1)S(1)} %get-tuple-element.168), channel_id=1, source_target_pairs={{0,4},{1,5},{2,6},{3,7},{4,8},{5,9},{6,10},{7,11},{8,12},{9,13},{1... | collective-permute-start | bytes 1572872 | tf_op jit(solution)/shard_map/cond/branch_1_fun/ppermute | solution.py:230
  72.2 18.3 %collective-permute-start.9 = (bf16[128,2048]{1,0:T(8,128)(2,1)S(1)}, bf16[128,2048]{1,0:T(8,128)(2,1)}, u32[]{:S(2)}, u32[]{:S(2)}) collective-permute-start(bf16[128,2048]{1,0:T(8,128)(2,1)S(1)} %get-tuple-element.169), channel_id=1, source_target_pairs={{4,0},{5,1},{6,2},{7,3},{8,4},{9,5},{10,6},{11,7},{12,8},{13,9},{1... | collective-permute-start | bytes 1572872 | tf_op jit(solution)/shard_map/cond/branch_1_fun/ppermute | solution.py:231
  90.5 15.7 %collective-permute-start = (bf16[128,2048]{1,0:T(8,128)(2,1)}, bf16[128,2048]{1,0:T(8,128)(2,1)}, u32[]{:S(2)}, u32[]{:S(2)}) collective-permute-start(bf16[128,2048]{1,0:T(8,128)(2,1)} %get-tuple-element.160), channel_id=1, source_target_pairs={{0,4},{1,5},{2,6},{3,7},{4,8},{5,9},{6,10},{7,11},{8,12},{9,13},{1... | collective-permute-start | bytes 1572872 | tf_op jit(solution)/shard_map/cond/branch_1_fun/ppermute | solution.py:230
  93.0 15.4 %collective-permute-start.1 = (bf16[128,2048]{1,0:T(8,128)(2,1)}, bf16[128,2048]{1,0:T(8,128)(2,1)}, u32[]{:S(2)}, u32[]{:S(2)}) collective-permute-start(bf16[128,2048]{1,0:T(8,128)(2,1)} %get-tuple-element.161), channel_id=1, source_target_pairs={{4,0},{5,1},{6,2},{7,3},{8,4},{9,5},{10,6},{11,7},{12,8},{13,9},{1... | collective-permute-start | bytes 1572872 | tf_op jit(solution)/shard_map/cond/branch_1_fun/ppermute | solution.py:231
  108.4 14.4 %collective-permute-start.70 = (bf16[128,2048]{1,0:T(8,128)(2,1)}, bf16[128,2048]{1,0:T(8,128)(2,1)S(1)}, u32[]{:S(2)}, u32[]{:S(2)}) collective-permute-start(bf16[128,2048]{1,0:T(8,128)(2,1)} %copy-done.16), channel_id=1, source_target_pairs={{0,3},{1,2},{2,1},{3,0},{4,7},{5,6},{6,5},{7,4},{8,11},{9,10},{10,... | collective-permute-start | bytes 1572872 | tf_op jit(solution)/shard_map/ppermute | solution.py:239
  128.1 1.3 copy-start.32
  129.4 4.8 %copy-start.3 = (bf16[128,2048]{1,0:T(8,128)(2,1)S(1)}, bf16[128,2048]{1,0:T(8,128)(2,1)}, u32[]{:S(2)}) copy-start(bf16[128,2048]{1,0:T(8,128)(2,1)} %copy-done.2) | copy-start | bytes 1572868
  131.5 22.2 %collective-permute-start.71 = (bf16[384,1024]{1,0:T(8,128)(2,1)}, bf16[384,1024]{1,0:T(8,128)(2,1)}, u32[]{:S(2)}, u32[]{:S(2)}) collective-permute-start(bf16[384,1024]{1,0:T(8,128)(2,1)} %broadcast_select_fusion.5), channel_id=1, source_target_pairs={{0,16},{16,0},{1,17},{17,1},{2,18},{18,2},{3,19},{19,3},{4,20},{20... | collective-permute-start | bytes 2359304 | tf_op jit(solution)/shard_map/ppermute | solution.py:57
  136.2 15.4 %collective-permute-start.32 = (bf16[128,2048]{1,0:T(8,128)(2,1)S(1)}, bf16[128,2048]{1,0:T(8,128)(2,1)}, u32[]{:S(2)}, u32[]{:S(2)}) collective-permute-start(bf16[128,2048]{1,0:T(8,128)(2,1)S(1)} %get-tuple-element.192), channel_id=1, source_target_pairs={{0,4},{1,5},{2,6},{3,7},{4,8},{5,9},{6,10},{7,11},{8,12},{9,13},{1... | collective-permute-start | bytes 1572872 | tf_op jit(solution)/shard_map/cond/branch_1_fun/ppermute | solution.py:230
  139.1 14.6 %collective-permute-start.33 = (bf16[128,2048]{1,0:T(8,128)(2,1)S(1)}, bf16[128,2048]{1,0:T(8,128)(2,1)}, u32[]{:S(2)}, u32[]{:S(2)}) collective-permute-start(bf16[128,2048]{1,0:T(8,128)(2,1)S(1)} %get-tuple-element.193), channel_id=1, source_target_pairs={{4,0},{5,1},{6,2},{7,3},{8,4},{9,5},{10,6},{11,7},{12,8},{13,9},{1... | collective-permute-start | bytes 1572872 | tf_op jit(solution)/shard_map/cond/branch_1_fun/ppermute | solution.py:231
  156.8 53.4 %all-to-all-start.2 = ((bf16[16,24,1536]{2,1,0:T(8,128)(2,1)}), bf16[16,24,1536]{2,1,0:T(8,128)(2,1)}, u32[]{:S(2)}, u32[]{:S(2)}) async-start(bf16[16,24,1536]{2,1,0:T(8,128)(2,1)} %bitcast.68), calls=%async_computation.2 | async-start | bytes 2359296 | tf_op jit(solution)/shard_map/all_to_all | solution.py:20
  163.4 40.2 %collective-permute-start.72 = (bf16[384,1024]{1,0:T(8,128)(2,1)}, bf16[384,1024]{1,0:T(8,128)(2,1)}, u32[]{:S(2)}, u32[]{:S(2)}) collective-permute-start(bf16[384,1024]{1,0:T(8,128)(2,1)} %bitcast.19), channel_id=1, source_target_pairs={{0,16},{16,0},{1,17},{17,1},{2,18},{18,2},{3,19},{19,3},{4,20},{20... | collective-permute-start | bytes 2359304 | tf_op jit(solution)/shard_map/ppermute | solution.py:43
  166.1 5.8 %copy-start.44 = (bf16[128,2048]{1,0:T(8,128)(2,1)S(1)}, bf16[128,2048]{1,0:T(8,128)(2,1)}, u32[]{:S(2)}) copy-start(bf16[128,2048]{1,0:T(8,128)(2,1)} %get-tuple-element.448) | copy-start | bytes 1572868
  166.1 5.8 %copy-start.45 = (bf16[128,2048]{1,0:T(8,128)(2,1)S(1)}, bf16[128,2048]{1,0:T(8,128)(2,1)}, u32[]{:S(2)}) copy-start(bf16[128,2048]{1,0:T(8,128)(2,1)} %get-tuple-element.449) | copy-start | bytes 1572868
  170.5 42.5 %collective-permute-start.73 = (bf16[128,2048]{1,0:T(8,128)(2,1)}, bf16[128,2048]{1,0:T(8,128)(2,1)}, u32[]{:S(2)}, u32[]{:S(2)}) collective-permute-start(bf16[128,2048]{1,0:T(8,128)(2,1)} %get-tuple-element.443), channel_id=1, source_target_pairs={{0,1},{1,0},{2,3},{3,2},{4,5},{5,4},{6,7},{7,6},{8,9},{9,8},{10,11... | collective-permute-start | bytes 1572872 | tf_op jit(solution)/shard_map/ppermute | solution.py:239
  170.5 42.5 %collective-permute-start.74 = (bf16[128,2048]{1,0:T(8,128)(2,1)}, bf16[128,2048]{1,0:T(8,128)(2,1)}, u32[]{:S(2)}, u32[]{:S(2)}) collective-permute-start(bf16[128,2048]{1,0:T(8,128)(2,1)} %get-tuple-element.444), channel_id=1, source_target_pairs={{0,2},{1,3},{2,0},{3,1},{4,6},{5,7},{6,4},{7,5},{8,10},{9,11},{10,... | collective-permute-start | bytes 1572872 | tf_op jit(solution)/shard_map/ppermute | solution.py:239
  171.9 28.9 %collective-permute-start.40 = (bf16[128,2048]{1,0:T(8,128)(2,1)S(1)}, bf16[128,2048]{1,0:T(8,128)(2,1)}, u32[]{:S(2)}, u32[]{:S(2)}) collective-permute-start(bf16[128,2048]{1,0:T(8,128)(2,1)S(1)} %get-tuple-element.200), channel_id=1, source_target_pairs={{0,4},{1,5},{2,6},{3,7},{4,8},{5,9},{6,10},{7,11},{8,12},{9,13},{1... | collective-permute-start | bytes 1572872 | tf_op jit(solution)/shard_map/cond/branch_1_fun/ppermute | solution.py:230
  175.3 27.5 %collective-permute-start.41 = (bf16[128,2048]{1,0:T(8,128)(2,1)S(1)}, bf16[128,2048]{1,0:T(8,128)(2,1)}, u32[]{:S(2)}, u32[]{:S(2)}) collective-permute-start(bf16[128,2048]{1,0:T(8,128)(2,1)S(1)} %get-tuple-element.201), channel_id=1, source_target_pairs={{4,0},{5,1},{6,2},{7,3},{8,4},{9,5},{10,6},{11,7},{12,8},{13,9},{1... | collective-permute-start | bytes 1572872 | tf_op jit(solution)/shard_map/cond/branch_1_fun/ppermute | solution.py:231
  202.8 2.2 copy-start.33
  202.8 14.5 %collective-permute-start.75 = (bf16[128,2048]{1,0:T(8,128)(2,1)}, bf16[128,2048]{1,0:T(8,128)(2,1)}, u32[]{:S(2)}, u32[]{:S(2)}) collective-permute-start(bf16[128,2048]{1,0:T(8,128)(2,1)} %copy-done.19), channel_id=1, source_target_pairs={{0,3},{1,2},{2,1},{3,0},{4,7},{5,6},{6,5},{7,4},{8,11},{9,10},{10,... | collective-permute-start | bytes 1572872 | tf_op jit(solution)/shard_map/ppermute | solution.py:239
  205.1 2.2 copy-start.31
  207.3 4.0 %copy-start.27 = (bf16[384,1024]{1,0:T(8,128)(2,1)S(1)}, bf16[384,1024]{1,0:T(8,128)(2,1)}, u32[]{:S(2)}) copy-start(bf16[384,1024]{1,0:T(8,128)(2,1)} %multiply_convert_fusion) | copy-start | bytes 2359300
  213.0 8.7 %copy-start.29 = (bf16[384,2048]{1,0:T(8,128)(2,1)S(1)}, bf16[384,2048]{1,0:T(8,128)(2,1)}, u32[]{:S(2)}) copy-start(bf16[384,2048]{1,0:T(8,128)(2,1)} %convolution_convert_fusion) | copy-start | bytes 4718596
  217.3 6.0 %copy-start.38 = (bf16[128,2048]{1,0:T(8,128)(2,1)S(1)}, bf16[128,2048]{1,0:T(8,128)(2,1)}, u32[]{:S(2)}) copy-start(bf16[128,2048]{1,0:T(8,128)(2,1)} %get-tuple-element.463) | copy-start | bytes 1572868
  217.3 31.3 %all-to-all-start.3 = ((bf16[16,24,1536]{2,1,0:T(8,128)(2,1)}), bf16[16,24,1536]{2,1,0:T(8,128)(2,1)}, u32[]{:S(2)}, u32[]{:S(2)}) async-start(bf16[16,24,1536]{2,1,0:T(8,128)(2,1)} %reorder.1), calls=%async_computation.3 | async-start | bytes 2359296 | tf_op jit(solution)/shard_map/all_to_all | solution.py:20
  222.7 19.9 %collective-permute-start.76 = (bf16[384,1024]{1,0:T(8,128)(2,1)}, bf16[384,1024]{1,0:T(8,128)(2,1)}, u32[]{:S(2)}, u32[]{:S(2)}) collective-permute-start(bf16[384,1024]{1,0:T(8,128)(2,1)} %broadcast_select_fusion.2), channel_id=1, source_target_pairs={{0,16},{16,0},{1,17},{17,1},{2,18},{18,2},{3,19},{19,3},{4,20},{20... | collective-permute-start | bytes 2359304 | tf_op jit(solution)/shard_map/ppermute | solution.py:57
  223.2 1.2 copy-start.34
  223.2 1.4 copy-start.36
  223.2 1.4 copy-start.39
  224.6 1.4 copy-start.4
  226.0 3.5 %copy-start.51 = (f32[128]{0:T(128)S(1)}, f32[128]{0:T(128)}, u32[]{:S(2)}) copy-start(f32[128]{0:T(128)} %copy-done.50) | copy-start | bytes 1540
  227.9 3.1 %copy-start.21 = (bf16[128,2048]{1,0:T(8,128)(2,1)}, bf16[128,2048]{1,0:T(8,128)(2,1)S(1)}, u32[]{:S(2)}) copy-start(bf16[128,2048]{1,0:T(8,128)(2,1)S(1)} %get-tuple-element.482) | copy-start | bytes 1572868
  227.9 3.1 %copy-start.24 = (bf16[128,2048]{1,0:T(8,128)(2,1)}, bf16[128,2048]{1,0:T(8,128)(2,1)S(1)}, u32[]{:S(2)}) copy-start(bf16[128,2048]{1,0:T(8,128)(2,1)S(1)} %get-tuple-element.481) | copy-start | bytes 1572868
  227.9 2.0 copy-start.49
  227.9 14.6 %copy-start.30 = (bf16[384,2048]{1,0:T(8,128)(2,1)S(1)}, bf16[384,2048]{1,0:T(8,128)(2,1)}, u32[]{:S(2)}) copy-start(bf16[384,2048]{1,0:T(8,128)(2,1)} %convolution_convert_fusion) | copy-start | bytes 4718596
  231.0 22.7 %copy-start.14 = (bf16[128,2048]{1,0:T(8,128)(2,1)S(1)}, bf16[128,2048]{1,0:T(8,128)(2,1)}, u32[]{:S(2)}) copy-start(bf16[128,2048]{1,0:T(8,128)(2,1)} %copy-done.13) | copy-start | bytes 1572868
  242.5 6.1 %copy-start.25 = (bf16[128,2048]{1,0:T(8,128)(2,1)S(1)}, bf16[128,2048]{1,0:T(8,128)(2,1)}, u32[]{:S(2)}) copy-start(bf16[128,2048]{1,0:T(8,128)(2,1)} %copy-done.24) | copy-start | bytes 1572868
  242.5 8.1 %copy-start.22 = (bf16[128,2048]{1,0:T(8,128)(2,1)S(1)}, bf16[128,2048]{1,0:T(8,128)(2,1)}, u32[]{:S(2)}) copy-start(bf16[128,2048]{1,0:T(8,128)(2,1)} %copy-done.21) | copy-start | bytes 1572868
  248.6 14.3 %collective-permute-start.78 = (bf16[128,2048]{1,0:T(8,128)(2,1)S(1)}, bf16[128,2048]{1,0:T(8,128)(2,1)S(1)}, u32[]{:S(2)}, u32[]{:S(2)}) collective-permute-start(bf16[128,2048]{1,0:T(8,128)(2,1)S(1)} %copy-done.25), channel_id=1, source_target_pairs={{0,3},{1,2},{2,1},{3,0},{4,7},{5,6},{6,5},{7,4},{8,11},{9,10},{10,... | collective-permute-start | bytes 1572872 | tf_op jit(solution)/shard_map/ppermute | solution.py:239
  250.7 30.2 %collective-permute-start.79 = (bf16[128,2048]{1,0:T(8,128)(2,1)S(1)}, bf16[128,2048]{1,0:T(8,128)(2,1)}, u32[]{:S(2)}, u32[]{:S(2)}) collective-permute-start(bf16[128,2048]{1,0:T(8,128)(2,1)S(1)} %copy-done.22), channel_id=1, source_target_pairs={{0,2},{1,3},{2,0},{3,1},{4,6},{5,7},{6,4},{7,5},{8,10},{9,11},{10,... | collective-permute-start | bytes 1572872 | tf_op jit(solution)/shard_map/ppermute | solution.py:239
  251.0 29.8 %collective-permute-start.80 = (bf16[128,2048]{1,0:T(8,128)(2,1)S(1)}, bf16[128,2048]{1,0:T(8,128)(2,1)}, u32[]{:S(2)}, u32[]{:S(2)}) collective-permute-start(bf16[128,2048]{1,0:T(8,128)(2,1)S(1)} %get-tuple-element.483), channel_id=1, source_target_pairs={{0,1},{1,0},{2,3},{3,2},{4,5},{5,4},{6,7},{7,6},{8,9},{9,8},{10,11... | collective-permute-start | bytes 1572872 | tf_op jit(solution)/shard_map/ppermute | solution.py:239
  253.1 29.2 %collective-permute-start.77 = (bf16[384,1024]{1,0:T(8,128)(2,1)}, bf16[384,1024]{1,0:T(8,128)(2,1)}, u32[]{:S(2)}, u32[]{:S(2)}) collective-permute-start(bf16[384,1024]{1,0:T(8,128)(2,1)} %slice.87), channel_id=1, source_target_pairs={{0,16},{16,0},{1,17},{17,1},{2,18},{18,2},{3,19},{19,3},{4,20},{20... | collective-permute-start | bytes 2359304 | tf_op jit(solution)/shard_map/ppermute | solution.py:43
  256.6 34.2 %all-to-all-start.4 = ((bf16[16,24,1024]{2,1,0:T(8,128)(2,1)}), bf16[16,24,1024]{2,1,0:T(8,128)(2,1)}, u32[]{:S(2)}, u32[]{:S(2)}) async-start(bf16[16,24,1024]{2,1,0:T(8,128)(2,1)} %bitcast.73), calls=%async_computation.4 | async-start | bytes 1572864 | tf_op jit(solution)/shard_map/all_to_all | solution.py:20
  282.2 1.7 copy-start.40
  282.2 1.7 copy-start.41
  282.2 1.8 copy-start.42
  282.2 2.0 copy-start.43
  284.2 8.8 %copy-start.1 = (bf16[1,512,2048]{2,1,0:T(8,128)(2,1)S(1)}, bf16[1,512,2048]{2,1,0:T(8,128)(2,1)}, u32[]{:S(2)}) copy-start(bf16[1,512,2048]{2,1,0:T(8,128)(2,1)} %param.55) | copy-start | bytes 6291460
  (19 other events, 16.8 us)
where the time goes:
time: 298 us; the launch traced here: 293 us
  waiting for transfers between devices  132 us (44%)
  starting transfers between devices  66.9 us (22%)
  local copies, waits for them, and re-layouts  33.2 us (11%)
  matrix products  23.7 us (8%)
  other arithmetic  19.9 us (7%)
  Pallas kernels  13.1 us (4%)
  between operations  3.68 us (1%)
    ppermute x12, waiting for transfers between devices, hand_over(): lax.ppermute(pieces[offset], 'expert', within_plane(offset))  56.6 us
    ppermute x4, waiting for transfers between devices, run(): lax.ppermute(up, 'expert', between_planes(moves))  52.4 us
    all_to_all x5, starting transfers between devices, exchange(): lax.all_to_all(blocks, 'expert', split_axis=0, concat_axis=0, tiled=True)  27.6 us
    unnamed x109, local copies, waits for them, and re-layouts  27.1 us
    ppermute x4, starting transfers between devices, run(): lax.ppermute(down, 'expert', between_planes([(b, a) for a, b in moves]))  15 us
    ppermute x2, waiting for transfers between devices, scatter_sum(): other = lax.ppermute(send, 'dp', ((0, 1), (1, 0)))  11.6 us
    ppermute x4, starting transfers between devices, run(): lax.ppermute(up, 'expert', between_planes(moves))  11.5 us
    pallas_call x4, Pallas kernels, choose(): pl.pallas_call(functools.partial(choose_kernel, len(options)), out_shape=...  9.2 us
  transfers between devices with their start and end apart: 30, of which 16 were waited for; matrix products, arithmetic and copies ran while one was open for 13% of the time, Pallas kernels for 4%

commit v1 on v0

--- a/solution.py
+++ b/solution.py
@@ -154,7 +154,7 @@
 
 def cut(arrays, member):
     rows, width = arrays[0].shape
-    anywhere = pl.BlockSpec(memory_space=pl.ANY)
+    anywhere = pl.BlockSpec(memory_space=pltpu.HBM)
     piece = (rows // GROUP, width)
     amount = GROUP * len(arrays)
     pieces = pl.pallas_call(
@@ -198,7 +198,7 @@
 
 
 def choose(choice, options):
-    anywhere = pl.BlockSpec(memory_space=pl.ANY)
+    anywhere = pl.BlockSpec(memory_space=pltpu.HBM)
     shape, dtype = options[0].shape, options[0].dtype
     amount = choice.shape[0]
     return pl.pallas_call(
@@ -224,29 +224,59 @@
     return [(GROUP * a + index, GROUP * b + index) for a, b in moves for index in range(GROUP)]
 
 
-def swap_round(moves):
-    def run(up, down):
+def swap_round(kind, up, down):
+    if kind == 0:
+        return up, down
+    moves = KINDS[kind - 1]
+    return (
+        lax.ppermute(up, "expert", between_planes(moves)),
+        lax.ppermute(down, "expert", between_planes([(b, a) for a, b in moves])),
+    )
+
+
+def swap_rounds(first_kind, second_kind):
+    def run(first_up, first_down, second_up, second_down):
         return (
-            lax.ppermute(up, "expert", between_planes(moves)),
-            lax.ppermute(down, "expert", between_planes([(b, a) for a, b in moves])),
+            *swap_round(first_kind, first_up, first_down),
+            *swap_round(second_kind, second_up, second_down),
         )
 
     return run
 
 
 def hand_over(pieces):
-    return list(pieces[:1]) + [
-        lax.ppermute(pieces[offset], "expert", within_plane(offset)) for offset in range(1, GROUP)
-    ]
-
-
-def swap_pieces(turn, plan, ways):
+    moved = {
+        offset: lax.ppermute(pieces[offset], "expert", within_plane(offset))
+        for offset in reversed(range(1, GROUP))
+    }
+    return [pieces[0]] + [moved[offset] for offset in range(1, GROUP)]
+
+
+def swap_one(turn, plan, ways):
     return list(
         lax.switch(
             plan[KIND_ROW + turn],
-            [lambda up, down: (up, down)] + [swap_round(moves) for moves in KINDS],
+            [functools.partial(swap_round, kind) for kind in range(len(KINDS) + 1)],
             ways[turn],
             ways[PLANES + turn],
+        )
+    )
+
+
+def swap_two(plan, ways):
+    first, second = plan[KIND_ROW], plan[KIND_ROW + 1]
+    amount = len(KINDS) + 1
+    branches = [swap_rounds(0, 0)] + [
+        swap_rounds(a, b) for a in range(1, amount) for b in range(amount)
+    ]
+    return list(
+        lax.switch(
+            jnp.where(first == 0, 0, 1 + (first - 1) * amount + second),
+            branches,
+            ways[0],
+            ways[PLANES],
+            ways[1],
+            ways[PLANES + 1],
         )
     )
 
@@ -324,7 +354,7 @@
         )
         held_b = hand_over(pieces_b)
         ways_a = choose(plan[UP_ROW:FINAL_ROW], held_a)
-        arrived_a = swap_pieces(0, plan, ways_a) + swap_pieces(1, plan, ways_a)
+        arrived_a = swap_two(plan, ways_a)
     grad_blocks = row_grads.reshape(experts, per_expert, part_width)
     here_grads = exchange(grad_blocks)
     expert_in = jnp.concatenate(gather_features(here_tokens.reshape(slots, part_width)), axis=1)
@@ -341,9 +371,9 @@
 
     if swaps:
         hidden, partial_out, ways_a, held_b = fence(hidden, partial_out, ways_a, held_b)
-        arrived_a += swap_pieces(2, plan, ways_a) + swap_pieces(3, plan, ways_a)
+        arrived_a += swap_one(2, plan, ways_a) + swap_one(3, plan, ways_a)
         ways_b = choose(plan[UP_ROW:FINAL_ROW], held_b)
-        arrived_b = swap_pieces(0, plan, ways_b)
+        arrived_b = swap_two(plan, ways_b)
     summed_out = scatter_sum(partial_out)
 
     if swaps:
@@ -351,7 +381,8 @@
             summed_out, here_grads, arrived_a, arrived_b, ways_b
         )
         own_a = hand_over(choose(plan[FINAL_ROW:], [*held_a, *arrived_a]))
-        arrived_b += swap_pieces(1, plan, ways_b)
+        arrived_b += swap_one(2, plan, ways_b) + swap_one(3, plan, ways_b)
+        ready_b = choose(plan[FINAL_ROW:], [*held_b, *arrived_b])
     back = exchange(
         jnp.concatenate([summed_out, hidden], axis=1).reshape(experts, per_expert, -1)
     )
@@ -368,11 +399,8 @@
     to_move = reorder(jnp.concatenate([back[:, :, part_width:], grad_blocks], axis=2), source)
 
     if swaps:
-        to_move, partial_in, own_a, arrived_b, ways_b = fence(
-            to_move, partial_in, own_a, arrived_b, ways_b
-        )
-        arrived_b += swap_pieces(2, plan, ways_b) + swap_pieces(3, plan, ways_b)
-        ready_b = choose(plan[FINAL_ROW:], [*held_b, *arrived_b])
+        to_move, partial_in, own_a, ready_b = fence(to_move, partial_in, own_a, ready_b)
+        own_b = hand_over(ready_b)
     there = exchange(to_move).reshape(slots, hidden_part + part_width)
     summed_in = scatter_sum(partial_in)
     back_out = back[:, :, :part_width].reshape(slots, part_width)
@@ -382,8 +410,7 @@
     ).astype(jnp.bfloat16)
 
     if swaps:
-        there, summed_in, ready_b, layer_out = fence(there, summed_in, ready_b, layer_out)
-        own_b = hand_over(ready_b)
+        there, summed_in, own_b, layer_out = fence(there, summed_in, own_b, layer_out)
     back_in = exchange(summed_in.reshape(experts, per_expert, part_width))
     token_grad = jnp.dot(
         plain, back_in.reshape(slots, part_width), preferred_element_type=jnp.float32

time: 298 us -> 328 us (1.10)
  starting transfers between devices: 66.9 us -> 117 us
  waiting for transfers between devices: 132 us -> 115 us
    ppermute x8 -> x12, starting transfers between devices: 26.5 us -> 75.2 us  [the longest x6 64.1 us: swap_round(): lax.ppermute(up, 'expert', between_planes(moves))]
    ppermute x8 -> x12, waiting for transfers between devices: 60.8 us -> 36.1 us  [the longest x6 34.9 us: swap_round(): lax.ppermute(up, 'expert', between_planes(moves))]
    ppermute x3, waiting for transfers between devices: 0.01 us -> 14.4 us  [gather_features(): other = lax.ppermute(rows, 'dp', ((0, 1), (1, 0)))]
    ppermute x12, waiting for transfers between devices: 56.6 us -> 49.3 us  [hand_over(): lax.ppermute(pieces[offset], 'expert', within_plane(offset))]
    unnamed x109 -> x103, local copies, waits for them, and re-layouts: 27.1 us -> 23.1 us
    all_to_all x5, waiting for transfers between devices: 3.51 us -> 0.05 us  [exchange(): lax.all_to_all(blocks, 'expert', split_axis=0, concat_axis=0, tiled=True)]
  transfers between devices with their start and end apart: 30 -> 34, of which waited for: 16 -> 12; matrix products, arithmetic and copies ran while one was open for 13% -> 13% of each run, Pallas kernels for 4% -> 4%
where the time goes in v1:
time: 328 us; the launch traced here: 325 us
  starting transfers between devices  117 us (36%)
  waiting for transfers between devices  115 us (35%)
  local copies, waits for them, and re-layouts  31.2 us (10%)
  matrix products  22.5 us (7%)
  other arithmetic  21.8 us (7%)
  Pallas kernels  12.9 us (4%)
  between operations  4.55 us (1%)
    ppermute x6, starting transfers between devices, swap_round(): lax.ppermute(up, 'expert', between_planes(moves))  64.1 us
    ppermute x12, waiting for transfers between devices, hand_over(): lax.ppermute(pieces[offset], 'expert', within_plane(offset))  49.3 us
    ppermute x6, waiting for transfers between devices, swap_round(): lax.ppermute(up, 'expert', between_planes(moves))  34.9 us
    all_to_all x5, starting transfers between devices, exchange(): lax.all_to_all(blocks, 'expert', split_axis=0, concat_axis=0, tiled=True)  28.9 us
    unnamed x103, local copies, waits for them, and re-layouts  23.1 us
    ppermute x2, waiting for transfers between devices, scatter_sum(): other = lax.ppermute(send, 'dp', ((0, 1), (1, 0)))  14.8 us
    ppermute x3, waiting for transfers between devices, gather_features(): other = lax.ppermute(rows, 'dp', ((0, 1), (1, 0)))  14.4 us
    ppermute x6, starting transfers between devices, swap_round(): lax.ppermute(down, 'expert', between_planes([(b, a) for a, b in moves]))  11.1 us
  transfers between devices with their start and end apart: 34, of which 12 were waited for; matrix products, arithmetic and copies ran while one was open for 13% of the time, Pallas kernels for 4%

profile of v1, /device:TPU:8, one launch (start us, length us, event | category | flops | bytes accessed | tf_op | source)
XLA Modules:
  0.0 325.4 jit_solution(4087788361368178949)
XLA Ops:
  3.1 2.3 convolution_convert_fusion.2
  5.4 1.6 copy-done.11
  7.0 1.6 copy-done.12
  14.1 6.3 %all-to-all-start = ((bf16[16,24,1024]{2,1,0:T(8,128)(2,1)}), bf16[16,24,1024]{2,1,0:T(8,128)(2,1)}, u32[]{:S(2)}, u32[]{:S(2)}) async-start(bf16[16,24,1024]{2,1,0:T(8,128)(2,1)} %bitcast.71), calls=%async_computation | async-start | bytes 1572864 | tf_op jit(solution)/shard_map/all_to_all | solution.py:20
  20.6 1.5 collective-permute-start.177
  22.4 5.4 %copy.22 = bf16[256,8,2,512]{3,1,2,0:T(8,128)(2,1)} copy(bf16[256,8,2,512]{3,2,1,0:T(2,128)(2,1)} %bitcast.68) | data formatting | bytes 8388608
  28.7 1.5 plan.1
  30.2 1.4 multiply_convert_fusion
  31.5 11.8 %collective-permute-done.177.refs_2_ = bf16[128,2048]{1,0:T(8,128)(2,1)} collective-permute-done((bf16[128,2048]{1,0:T(8,128)(2,1)}, bf16[128,2048]{1,0:T(8,128)(2,1)}, u32[]{:S(2)}, u32[]{:S(2)}) %collective-permute-start.177) | collective-permute-done | bytes 524320 | tf_op jit(solution)/shard_map/ppermute | solution.py:249
  43.3 10.3 %collective-permute-done.178.refs_3_ = bf16[128,2048]{1,0:T(8,128)(2,1)} collective-permute-done((bf16[128,2048]{1,0:T(8,128)(2,1)}, bf16[128,2048]{1,0:T(8,128)(2,1)}, u32[]{:S(2)}, u32[]{:S(2)}) %collective-permute-start.178) | collective-permute-done | bytes 524320 | tf_op jit(solution)/shard_map/ppermute | solution.py:249
  53.6 5.1 %all-to-all-start.1 = ((bf16[16,24,1024]{2,1,0:T(8,128)(2,1)}), bf16[16,24,1024]{2,1,0:T(8,128)(2,1)}, u32[]{:S(2)}, u32[]{:S(2)}) async-start(bf16[16,24,1024]{2,1,0:T(8,128)(2,1)} %bitcast.63), calls=%async_computation.1 | async-start | bytes 1572864 | tf_op jit(solution)/shard_map/all_to_all | solution.py:20
  58.8 1.5 collective-permute-start.179
  63.0 2.6 choose.4
  65.6 6.1 %conditional.6 = (bf16[128,2048]{1,0:T(8,128)(2,1)}, bf16[128,2048]{1,0:T(8,128)(2,1)}, bf16[128,2048]{1,0:T(8,128)(2,1)}, bf16[128,2048]{1,0:T(8,128)(2,1)}) conditional(s32[]{:T(128)} %bitcast.13, (bf16[128,2048]{1,0:T(8,128)(2,1)S(1)}, bf16[128,2048]{1,0:T(8,128)(2,1)S(1)}, bf16[128,2048]{1,0:T(8,128)(2,1)S(1)}, ...), branch_computations={%region_3.4_spmd, %region_4.5_spmd, %region_5.6_spmd, %region_6.7_... | conditional | bytes 8388800 | solution.py:273
  65.6 1.5 collective-permute-start.60
  67.1 1.5 collective-permute-start.61
  68.6 1.5 collective-permute-start.62
  70.0 1.5 collective-permute-start.63
  71.8 1.5 collective-permute-start.181
  73.6 5.0 %collective-permute-done.179 = bf16[384,1024]{1,0:T(8,128)(2,1)} collective-permute-done((bf16[384,1024]{1,0:T(8,128)(2,1)}, bf16[384,1024]{1,0:T(8,128)(2,1)}, u32[]{:S(2)}, u32[]{:S(2)}) %collective-permute-start.179) | collective-permute-done | bytes 786464 | tf_op jit(solution)/shard_map/ppermute | solution.py:43
  78.7 1.5 broadcast_select_fusion.7
  80.2 1.2 pad_maximum_fusion.2
  82.2 5.1 %collective-permute-done.181.refs_2_ = bf16[128,2048]{1,0:T(8,128)(2,1)S(1)} collective-permute-done((bf16[128,2048]{1,0:T(8,128)(2,1)}, bf16[128,2048]{1,0:T(8,128)(2,1)S(1)}, u32[]{:S(2)}, u32[]{:S(2)}) %collective-permute-start.181) | collective-permute-done | bytes 524320 | tf_op jit(solution)/shard_map/ppermute | solution.py:249
  88.1 10.1 %collective-permute-done.182.refs_3_ = bf16[128,2048]{1,0:T(8,128)(2,1)S(1)} collective-permute-done((bf16[128,2048]{1,0:T(8,128)(2,1)}, bf16[128,2048]{1,0:T(8,128)(2,1)S(1)}, u32[]{:S(2)}, u32[]{:S(2)}) %collective-permute-start.182) | collective-permute-done | bytes 524320 | tf_op jit(solution)/shard_map/ppermute | solution.py:249
  99.0 4.4 %fusion.44 = f32[384,1024]{1,0:T(8,128)S(1)} fusion(bf16[384,2048]{1,0:T(8,128)(2,1)} %pad_maximum_fusion.2, bf16[2048,1024]{1,0:T(8,128)(2,1)} %bitcast.69), kind=kOutput, calls=%fused_computation.96 | convolution fusion | flops 1610612736 | bytes 7340032 | tf_op jit(solution)/shard_map/dot_general | solution.py:365
  105.8 1.5 collective-permute-start.183
  108.6 1.8 choose.5
  110.4 5.9 %conditional.9 = (bf16[128,2048]{1,0:T(8,128)(2,1)}, bf16[128,2048]{1,0:T(8,128)(2,1)}, bf16[128,2048]{1,0:T(8,128)(2,1)}, bf16[128,2048]{1,0:T(8,128)(2,1)}) conditional(s32[]{:T(128)} %bitcast.13, (bf16[128,2048]{1,0:T(8,128)(2,1)S(1)}, bf16[128,2048]{1,0:T(8,128)(2,1)S(1)}, bf16[128,2048]{1,0:T(8,128)(2,1)S(1)}, ...), branch_computations={%region_34.35_spmd, %region_35.36_spmd, %region_36.37_spmd, %regio... | conditional | bytes 8388800 | solution.py:273
  110.5 1.5 collective-permute-start.148
  111.9 1.5 collective-permute-start.149
  113.4 1.5 collective-permute-start.150
  114.8 1.4 collective-permute-start.151
  116.3 70.3 %conditional.7 = ((bf16[128,2048]{1,0:T(8,128)(2,1)}, bf16[128,2048]{1,0:T(8,128)(2,1)})) conditional(s32[]{:T(128)} %bitcast.15, (bf16[128,2048]{1,0:T(8,128)(2,1)}, bf16[128,2048]{1,0:T(8,128)(2,1)}) %tuple.262, (bf16[128,2048]{1,0:T(8,128)(2,1)}, bf16[128,2048]{1,0:T(8,128)(2,1)}) %tuple.262, ...), branch_computations={%region_24.25_spmd, %region_25.26_spmd, %region_26.27_spmd, %regio... | conditional | bytes 6291560 | solution.py:257
  116.4 53.8 %collective-permute-start.76 = (bf16[128,2048]{1,0:T(8,128)(2,1)}, bf16[128,2048]{1,0:T(8,128)(2,1)S(1)}, u32[]{:S(2)}, u32[]{:S(2)}) collective-permute-start(bf16[128,2048]{1,0:T(8,128)(2,1)} %get-tuple-element.500), channel_id=1, source_target_pairs={{0,4},{1,5},{2,6},{3,7},{4,12},{5,13},{6,14},{7,15},{16,20},{17,21... | collective-permute-start | bytes 1572872 | tf_op jit(solution)/shard_map/cond/branch_3_fun/ppermute | solution.py:232
  170.2 3.3 %collective-permute-start.77 = (bf16[128,2048]{1,0:T(8,128)(2,1)}, bf16[128,2048]{1,0:T(8,128)(2,1)S(1)}, u32[]{:S(2)}, u32[]{:S(2)}) collective-permute-start(bf16[128,2048]{1,0:T(8,128)(2,1)} %get-tuple-element.501), channel_id=1, source_target_pairs={{4,0},{5,1},{6,2},{7,3},{12,4},{13,5},{14,6},{15,7},{20,16},{21,17... | collective-permute-start | bytes 1572872 | tf_op jit(solution)/shard_map/cond/branch_3_fun/ppermute | solution.py:233
  173.5 10.3 %collective-permute-done.76 = bf16[128,2048]{1,0:T(8,128)(2,1)S(1)} collective-permute-done((bf16[128,2048]{1,0:T(8,128)(2,1)}, bf16[128,2048]{1,0:T(8,128)(2,1)S(1)}, u32[]{:S(2)}, u32[]{:S(2)}) %collective-permute-start.76) | collective-permute-done | bytes 524320 | tf_op jit(solution)/shard_map/cond/branch_3_fun/ppermute | solution.py:232
  186.6 2.0 add_convert_fusion.1
  189.8 5.8 %all-to-all-start.2 = ((bf16[16,24,1536]{2,1,0:T(8,128)(2,1)}), bf16[16,24,1536]{2,1,0:T(8,128)(2,1)}, u32[]{:S(2)}, u32[]{:S(2)}) async-start(bf16[16,24,1536]{2,1,0:T(8,128)(2,1)} %bitcast.67), calls=%async_computation.2 | async-start | bytes 2359296 | tf_op jit(solution)/shard_map/all_to_all | solution.py:20
  196.3 2.7 choose.6
  200.6 1.5 collective-permute-start.186
  202.1 32.5 %conditional.10 = ((bf16[128,2048]{1,0:T(8,128)(2,1)}, bf16[128,2048]{1,0:T(8,128)(2,1)})) conditional(s32[]{:T(128)} %bitcast.15, (bf16[128,2048]{1,0:T(8,128)(2,1)}, bf16[128,2048]{1,0:T(8,128)(2,1)}) %tuple.266, (bf16[128,2048]{1,0:T(8,128)(2,1)}, bf16[128,2048]{1,0:T(8,128)(2,1)}) %tuple.266, ...), branch_computations={%region_55.56_spmd, %region_56.57_spmd, %region_57.58_spmd, %regio... | conditional | bytes 6291560 | solution.py:257
  202.1 4.4 %collective-permute-start.164 = (bf16[128,2048]{1,0:T(8,128)(2,1)}, bf16[128,2048]{1,0:T(8,128)(2,1)S(1)}, u32[]{:S(2)}, u32[]{:S(2)}) collective-permute-start(bf16[128,2048]{1,0:T(8,128)(2,1)} %get-tuple-element.596), channel_id=1, source_target_pairs={{0,4},{1,5},{2,6},{3,7},{4,12},{5,13},{6,14},{7,15},{16,20},{17,21... | collective-permute-start | bytes 1572872 | tf_op jit(solution)/shard_map/cond/branch_3_fun/ppermute | solution.py:232
  206.5 1.9 collective-permute-start.165
  208.4 24.6 %collective-permute-done.164 = bf16[128,2048]{1,0:T(8,128)(2,1)S(1)} collective-permute-done((bf16[128,2048]{1,0:T(8,128)(2,1)}, bf16[128,2048]{1,0:T(8,128)(2,1)S(1)}, u32[]{:S(2)}, u32[]{:S(2)}) %collective-permute-start.164) | collective-permute-done | bytes 524320 | tf_op jit(solution)/shard_map/cond/branch_3_fun/ppermute | solution.py:232
  237.7 2.0 choose.7
  239.8 2.2 broadcast_select_fusion.4
  242.4 1.3 multiply_convert_fusion.2
  244.6 3.0 convolution_convert_fusion
  248.8 1.6 reorder.1
  250.4 7.1 %all-to-all-start.3 = ((bf16[16,24,1536]{2,1,0:T(8,128)(2,1)}), bf16[16,24,1536]{2,1,0:T(8,128)(2,1)}, u32[]{:S(2)}, u32[]{:S(2)}) async-start(bf16[16,24,1536]{2,1,0:T(8,128)(2,1)} %reorder.1), calls=%async_computation.3 | async-start | bytes 2359296 | tf_op jit(solution)/shard_map/all_to_all | solution.py:20
  257.6 2.3 broadcast_select_fusion.2
  260.5 1.5 collective-permute-start.190
  262.4 1.2 slice.91
  265.0 14.8 %collective-permute-done.188 = bf16[384,1024]{1,0:T(8,128)(2,1)} collective-permute-done((bf16[384,1024]{1,0:T(8,128)(2,1)}, bf16[384,1024]{1,0:T(8,128)(2,1)}, u32[]{:S(2)}, u32[]{:S(2)}) %collective-permute-start.188) | collective-permute-done | bytes 786464 | tf_op jit(solution)/shard_map/ppermute | solution.py:57
  279.8 2.5 add_convert_fusion
  283.9 11.4 %collective-permute-done.191 = bf16[128,2048]{1,0:T(8,128)(2,1)} collective-permute-done((bf16[128,2048]{1,0:T(8,128)(2,1)S(1)}, bf16[128,2048]{1,0:T(8,128)(2,1)}, u32[]{:S(2)}, u32[]{:S(2)}) %collective-permute-start.191) | collective-permute-done | bytes 524320 | tf_op jit(solution)/shard_map/ppermute | solution.py:249
  295.3 1.2 slice.87
  296.5 1.2 collective-permute-start.192
  297.7 3.0 broadcast_select_fusion.23
  300.6 4.6 %all-to-all-start.4 = ((bf16[16,24,1024]{2,1,0:T(8,128)(2,1)}), bf16[16,24,1024]{2,1,0:T(8,128)(2,1)S(1)}, u32[]{:S(2)}, u32[]{:S(2)}) async-start(bf16[16,24,1024]{2,1,0:T(8,128)(2,1)} %bitcast.22), calls=%async_computation.4 | async-start | bytes 1572864 | tf_op jit(solution)/shard_map/all_to_all | solution.py:20
  305.2 1.5 broadcast_select_fusion.19
  306.8 9.4 %collective-permute-done.192 = bf16[384,1024]{1,0:T(8,128)(2,1)} collective-permute-done((bf16[384,1024]{1,0:T(8,128)(2,1)S(1)}, bf16[384,1024]{1,0:T(8,128)(2,1)}, u32[]{:S(2)}, u32[]{:S(2)}) %collective-permute-start.192) | collective-permute-done | bytes 786464 | tf_op jit(solution)/shard_map/ppermute | solution.py:43
  316.2 1.5 broadcast_select_fusion.1
  317.7 6.6 %fusion.3 = (bf16[1,512,2048]{2,1,0:T(8,128)(2,1)}, bf16[1,512,2048]{2,1,0:T(8,128)(2,1)}, bf16[1,512,2048]{2,1,0:T(8,128)(2,1)}) fusion(bf16[128,2048]{1,0:T(8,128)(2,1)S(1)} %get-tuple-element.873, bf16[128,2048]{1,0:T(8,128)(2,1)S(1)} %get-tuple-element.872, bf16[128,2048]{1,0:T(8,128)(2,1)S(1)} %get-tuple-element.871, ...), kind=kOutput, calls=%fused_computation.8 | convolution fusion | flops 837812224 | bytes 12451840 | tf_op jit(solution)/shard_map/dot_general | solution.py:425
  (171 shorter events, 33.4 us)
Async XLA Ops:
  0.6 103.1 %copy-start = (bf16[1,512,2048]{2,1,0:T(8,128)(2,1)S(1)}, bf16[1,512,2048]{2,1,0:T(8,128)(2,1)}, u32[]{:S(2)}) copy-start(bf16[1,512,2048]{2,1,0:T(8,128)(2,1)} %param.77) | copy-start | bytes 6291460
  8.6 13.7 %copy-start.49 = (f32[2,64,2]{1,2,0:T(2,128)S(1)}, f32[2,64,2]{1,2,0:T(2,128)}, u32[]{:S(2)}) copy-start(f32[2,64,2]{1,2,0:T(2,128)} %param.74) | copy-start | bytes 3076
  14.1 39.5 %all-to-all-start = ((bf16[16,24,1024]{2,1,0:T(8,128)(2,1)}), bf16[16,24,1024]{2,1,0:T(8,128)(2,1)}, u32[]{:S(2)}, u32[]{:S(2)}) async-start(bf16[16,24,1024]{2,1,0:T(8,128)(2,1)} %bitcast.71), calls=%async_computation | async-start | bytes 1572864 | tf_op jit(solution)/shard_map/all_to_all | solution.py:20
  20.4 11.1 %collective-permute-start.176 = (bf16[128,2048]{1,0:T(8,128)(2,1)}, bf16[128,2048]{1,0:T(8,128)(2,1)}, u32[]{:S(2)}, u32[]{:S(2)}) collective-permute-start(bf16[128,2048]{1,0:T(8,128)(2,1)} %copy-done.30), channel_id=1, source_target_pairs={{0,1},{1,0},{2,3},{3,2},{4,5},{5,4},{6,7},{7,6},{8,9},{9,8},{10,11... | collective-permute-start | bytes 1572872 | tf_op jit(solution)/shard_map/ppermute | solution.py:249
  20.6 22.8 %collective-permute-start.177 = (bf16[128,2048]{1,0:T(8,128)(2,1)}, bf16[128,2048]{1,0:T(8,128)(2,1)}, u32[]{:S(2)}, u32[]{:S(2)}) collective-permute-start(bf16[128,2048]{1,0:T(8,128)(2,1)} %copy-done.29), channel_id=1, source_target_pairs={{0,2},{1,3},{2,0},{3,1},{4,6},{5,7},{6,4},{7,5},{8,10},{9,11},{10,... | collective-permute-start | bytes 1572872 | tf_op jit(solution)/shard_map/ppermute | solution.py:249
  22.1 31.6 %collective-permute-start.178 = (bf16[128,2048]{1,0:T(8,128)(2,1)}, bf16[128,2048]{1,0:T(8,128)(2,1)}, u32[]{:S(2)}, u32[]{:S(2)}) collective-permute-start(bf16[128,2048]{1,0:T(8,128)(2,1)} %copy-done.28), channel_id=1, source_target_pairs={{0,3},{1,2},{2,1},{3,0},{4,7},{5,6},{6,5},{7,4},{8,11},{9,10},{10,... | collective-permute-start | bytes 1572872 | tf_op jit(solution)/shard_map/ppermute | solution.py:249
  22.4 5.4 %copy-start.45 = (f32[128]{0:T(128)}, f32[128]{0:T(128)S(1)}, u32[]{:S(2)}) copy-start(f32[128]{0:T(128)S(1)} %get-tuple-element.880) | copy-start | bytes 1540
  22.4 5.4 %copy-start.47 = (f32[128]{0:T(128)}, f32[128]{0:T(128)S(1)}, u32[]{:S(2)}) copy-start(f32[128]{0:T(128)S(1)} %get-tuple-element.881) | copy-start | bytes 1540
  22.4 7.7 %copy-start.43 = (bf16[2,64,1024]{2,1,0:T(8,128)(2,1)S(1)}, bf16[2,64,1024]{2,1,0:T(8,128)(2,1)}, u32[]{:S(2)}) copy-start(bf16[2,64,1024]{2,1,0:T(8,128)(2,1)} %param.72) | copy-start | bytes 786436
  30.1 30.1 %copy-start.44 = (s32[16]{0:T(128)S(1)}, s32[16]{0:T(128)}, u32[]{:S(2)}) copy-start(s32[16]{0:T(128)} %plan.1) | copy-start | bytes 196
  53.6 45.4 %all-to-all-start.1 = ((bf16[16,24,1024]{2,1,0:T(8,128)(2,1)}), bf16[16,24,1024]{2,1,0:T(8,128)(2,1)}, u32[]{:S(2)}, u32[]{:S(2)}) async-start(bf16[16,24,1024]{2,1,0:T(8,128)(2,1)} %bitcast.63), calls=%async_computation.1 | async-start | bytes 1572864 | tf_op jit(solution)/shard_map/all_to_all | solution.py:20
  58.8 19.9 %collective-permute-start.179 = (bf16[384,1024]{1,0:T(8,128)(2,1)}, bf16[384,1024]{1,0:T(8,128)(2,1)}, u32[]{:S(2)}, u32[]{:S(2)}) collective-permute-start(bf16[384,1024]{1,0:T(8,128)(2,1)} %bitcast.11), channel_id=1, source_target_pairs={{0,16},{16,0},{1,17},{17,1},{2,18},{18,2},{3,19},{19,3},{4,20},{20... | collective-permute-start | bytes 2359304 | tf_op jit(solution)/shard_map/ppermute | solution.py:43
  65.6 5.9 %collective-permute-start.60 = (bf16[128,2048]{1,0:T(8,128)(2,1)S(1)}, bf16[128,2048]{1,0:T(8,128)(2,1)}, u32[]{:S(2)}, u32[]{:S(2)}) collective-permute-start(bf16[128,2048]{1,0:T(8,128)(2,1)S(1)} %get-tuple-element.484), channel_id=1, source_target_pairs={{0,12},{1,13},{2,14},{3,15},{16,28},{17,29},{18,30},{19,31}} | collective-permute-start | bytes 1572872 | tf_op jit(solution)/shard_map/cond/branch_18_fun/ppermute | solution.py:232
  67.1 4.4 %collective-permute-start.61 = (bf16[128,2048]{1,0:T(8,128)(2,1)S(1)}, bf16[128,2048]{1,0:T(8,128)(2,1)}, u32[]{:S(2)}, u32[]{:S(2)}) collective-permute-start(bf16[128,2048]{1,0:T(8,128)(2,1)S(1)} %get-tuple-element.485), channel_id=1, source_target_pairs={{12,0},{13,1},{14,2},{15,3},{28,16},{29,17},{30,18},{31,19}} | collective-permute-start | bytes 1572872 | tf_op jit(solution)/shard_map/cond/branch_18_fun/ppermute | solution.py:233
  68.6 3.0 collective-permute-start.62
  70.0 1.5 collective-permute-start.63
  71.7 9.7 %collective-permute-start.180 = (bf16[128,2048]{1,0:T(8,128)(2,1)}, bf16[128,2048]{1,0:T(8,128)(2,1)S(1)}, u32[]{:S(2)}, u32[]{:S(2)}) collective-permute-start(bf16[128,2048]{1,0:T(8,128)(2,1)} %copy-done.20), channel_id=1, source_target_pairs={{0,1},{1,0},{2,3},{3,2},{4,5},{5,4},{6,7},{7,6},{8,9},{9,8},{10,11... | collective-permute-start | bytes 1572872 | tf_op jit(solution)/shard_map/ppermute | solution.py:249
  71.8 15.5 %collective-permute-start.181 = (bf16[128,2048]{1,0:T(8,128)(2,1)}, bf16[128,2048]{1,0:T(8,128)(2,1)S(1)}, u32[]{:S(2)}, u32[]{:S(2)}) collective-permute-start(bf16[128,2048]{1,0:T(8,128)(2,1)} %copy-done.19), channel_id=1, source_target_pairs={{0,2},{1,3},{2,0},{3,1},{4,6},{5,7},{6,4},{7,5},{8,10},{9,11},{10,... | collective-permute-start | bytes 1572872 | tf_op jit(solution)/shard_map/ppermute | solution.py:249
  73.3 24.9 %collective-permute-start.182 = (bf16[128,2048]{1,0:T(8,128)(2,1)}, bf16[128,2048]{1,0:T(8,128)(2,1)S(1)}, u32[]{:S(2)}, u32[]{:S(2)}) collective-permute-start(bf16[128,2048]{1,0:T(8,128)(2,1)} %copy-done.18), channel_id=1, source_target_pairs={{0,3},{1,2},{2,1},{3,0},{4,7},{5,6},{6,5},{7,4},{8,11},{9,10},{10,... | collective-permute-start | bytes 1572872 | tf_op jit(solution)/shard_map/ppermute | solution.py:249
  104.8 3.1 copy-start.32
  104.8 3.8 %copy-start.3 = (bf16[128,2048]{1,0:T(8,128)(2,1)S(1)}, bf16[128,2048]{1,0:T(8,128)(2,1)}, u32[]{:S(2)}) copy-start(bf16[128,2048]{1,0:T(8,128)(2,1)} %copy-done.2) | copy-start | bytes 1572868
  104.8 3.8 %copy-start.6 = (bf16[128,2048]{1,0:T(8,128)(2,1)S(1)}, bf16[128,2048]{1,0:T(8,128)(2,1)}, u32[]{:S(2)}) copy-start(bf16[128,2048]{1,0:T(8,128)(2,1)} %copy-done.5) | copy-start | bytes 1572868
  104.8 3.8 %copy-start.9 = (bf16[128,2048]{1,0:T(8,128)(2,1)S(1)}, bf16[128,2048]{1,0:T(8,128)(2,1)}, u32[]{:S(2)}) copy-start(bf16[128,2048]{1,0:T(8,128)(2,1)} %copy-done.8) | copy-start | bytes 1572868
  105.8 80.8 %collective-permute-start.183 = (bf16[384,1024]{1,0:T(8,128)(2,1)}, bf16[384,1024]{1,0:T(8,128)(2,1)}, u32[]{:S(2)}, u32[]{:S(2)}) collective-permute-start(bf16[384,1024]{1,0:T(8,128)(2,1)} %broadcast_select_fusion.5), channel_id=1, source_target_pairs={{0,16},{16,0},{1,17},{17,1},{2,18},{18,2},{3,19},{19,3},{4,20},{20... | collective-permute-start | bytes 2359304 | tf_op jit(solution)/shard_map/ppermute | solution.py:57
  110.5 5.8 %collective-permute-start.148 = (bf16[128,2048]{1,0:T(8,128)(2,1)S(1)}, bf16[128,2048]{1,0:T(8,128)(2,1)}, u32[]{:S(2)}, u32[]{:S(2)}) collective-permute-start(bf16[128,2048]{1,0:T(8,128)(2,1)S(1)} %get-tuple-element.580), channel_id=1, source_target_pairs={{0,12},{1,13},{2,14},{3,15},{16,28},{17,29},{18,30},{19,31}} | collective-permute-start | bytes 1572872 | tf_op jit(solution)/shard_map/cond/branch_18_fun/ppermute | solution.py:232
  111.9 4.4 %collective-permute-start.149 = (bf16[128,2048]{1,0:T(8,128)(2,1)S(1)}, bf16[128,2048]{1,0:T(8,128)(2,1)}, u32[]{:S(2)}, u32[]{:S(2)}) collective-permute-start(bf16[128,2048]{1,0:T(8,128)(2,1)S(1)} %get-tuple-element.581), channel_id=1, source_target_pairs={{12,0},{13,1},{14,2},{15,3},{28,16},{29,17},{30,18},{31,19}} | collective-permute-start | bytes 1572872 | tf_op jit(solution)/shard_map/cond/branch_18_fun/ppermute | solution.py:233
  113.4 2.9 collective-permute-start.150
  114.8 1.5 collective-permute-start.151
  116.4 67.5 %collective-permute-start.76 = (bf16[128,2048]{1,0:T(8,128)(2,1)}, bf16[128,2048]{1,0:T(8,128)(2,1)S(1)}, u32[]{:S(2)}, u32[]{:S(2)}) collective-permute-start(bf16[128,2048]{1,0:T(8,128)(2,1)} %get-tuple-element.500), channel_id=1, source_target_pairs={{0,4},{1,5},{2,6},{3,7},{4,12},{5,13},{6,14},{7,15},{16,20},{17,21... | collective-permute-start | bytes 1572872 | tf_op jit(solution)/shard_map/cond/branch_3_fun/ppermute | solution.py:232
  170.2 15.6 %collective-permute-start.77 = (bf16[128,2048]{1,0:T(8,128)(2,1)}, bf16[128,2048]{1,0:T(8,128)(2,1)S(1)}, u32[]{:S(2)}, u32[]{:S(2)}) collective-permute-start(bf16[128,2048]{1,0:T(8,128)(2,1)} %get-tuple-element.501), channel_id=1, source_target_pairs={{4,0},{5,1},{6,2},{7,3},{12,4},{13,5},{14,6},{15,7},{20,16},{21,17... | collective-permute-start | bytes 1572872 | tf_op jit(solution)/shard_map/cond/branch_3_fun/ppermute | solution.py:233
  189.8 57.9 %all-to-all-start.2 = ((bf16[16,24,1536]{2,1,0:T(8,128)(2,1)}), bf16[16,24,1536]{2,1,0:T(8,128)(2,1)}, u32[]{:S(2)}, u32[]{:S(2)}) async-start(bf16[16,24,1536]{2,1,0:T(8,128)(2,1)} %bitcast.67), calls=%async_computation.2 | async-start | bytes 2359296 | tf_op jit(solution)/shard_map/all_to_all | solution.py:20
  195.6 44.2 %collective-permute-start.184 = (bf16[384,1024]{1,0:T(8,128)(2,1)}, bf16[384,1024]{1,0:T(8,128)(2,1)}, u32[]{:S(2)}, u32[]{:S(2)}) collective-permute-start(bf16[384,1024]{1,0:T(8,128)(2,1)} %bitcast.18), channel_id=1, source_target_pairs={{0,16},{16,0},{1,17},{17,1},{2,18},{18,2},{3,19},{19,3},{4,20},{20... | collective-permute-start | bytes 2359304 | tf_op jit(solution)/shard_map/ppermute | solution.py:43
  200.6 49.8 %collective-permute-start.185 = (bf16[128,2048]{1,0:T(8,128)(2,1)}, bf16[128,2048]{1,0:T(8,128)(2,1)}, u32[]{:S(2)}, u32[]{:S(2)}) collective-permute-start(bf16[128,2048]{1,0:T(8,128)(2,1)} %get-tuple-element.825), channel_id=1, source_target_pairs={{0,1},{1,0},{2,3},{3,2},{4,5},{5,4},{6,7},{7,6},{8,9},{9,8},{10,11... | collective-permute-start | bytes 1572872 | tf_op jit(solution)/shard_map/ppermute | solution.py:249
  200.6 49.8 %collective-permute-start.186 = (bf16[128,2048]{1,0:T(8,128)(2,1)}, bf16[128,2048]{1,0:T(8,128)(2,1)}, u32[]{:S(2)}, u32[]{:S(2)}) collective-permute-start(bf16[128,2048]{1,0:T(8,128)(2,1)} %get-tuple-element.826), channel_id=1, source_target_pairs={{0,2},{1,3},{2,0},{3,1},{4,6},{5,7},{6,4},{7,5},{8,10},{9,11},{10,... | collective-permute-start | bytes 1572872 | tf_op jit(solution)/shard_map/ppermute | solution.py:249
  202.1 30.9 %collective-permute-start.164 = (bf16[128,2048]{1,0:T(8,128)(2,1)}, bf16[128,2048]{1,0:T(8,128)(2,1)S(1)}, u32[]{:S(2)}, u32[]{:S(2)}) collective-permute-start(bf16[128,2048]{1,0:T(8,128)(2,1)} %get-tuple-element.596), channel_id=1, source_target_pairs={{0,4},{1,5},{2,6},{3,7},{4,12},{5,13},{6,14},{7,15},{16,20},{17,21... | collective-permute-start | bytes 1572872 | tf_op jit(solution)/shard_map/cond/branch_3_fun/ppermute | solution.py:232
  206.5 27.3 %collective-permute-start.165 = (bf16[128,2048]{1,0:T(8,128)(2,1)}, bf16[128,2048]{1,0:T(8,128)(2,1)S(1)}, u32[]{:S(2)}, u32[]{:S(2)}) collective-permute-start(bf16[128,2048]{1,0:T(8,128)(2,1)} %get-tuple-element.597), channel_id=1, source_target_pairs={{4,0},{5,1},{6,2},{7,3},{12,4},{13,5},{14,6},{15,7},{20,16},{21,17... | collective-permute-start | bytes 1572872 | tf_op jit(solution)/shard_map/cond/branch_3_fun/ppermute | solution.py:233
  234.6 15.8 %collective-permute-start.187 = (bf16[128,2048]{1,0:T(8,128)(2,1)}, bf16[128,2048]{1,0:T(8,128)(2,1)}, u32[]{:S(2)}, u32[]{:S(2)}) collective-permute-start(bf16[128,2048]{1,0:T(8,128)(2,1)} %copy-done.21), channel_id=1, source_target_pairs={{0,3},{1,2},{2,1},{3,0},{4,7},{5,6},{6,5},{7,4},{8,11},{9,10},{10,... | collective-permute-start | bytes 1572872 | tf_op jit(solution)/shard_map/ppermute | solution.py:249
  239.7 3.9 %copy-start.15 = (bf16[128,2048]{1,0:T(8,128)(2,1)}, bf16[128,2048]{1,0:T(8,128)(2,1)S(1)}, u32[]{:S(2)}) copy-start(bf16[128,2048]{1,0:T(8,128)(2,1)S(1)} %get-tuple-element.860) | copy-start | bytes 1572868
  239.7 3.9 %copy-start.22 = (bf16[128,2048]{1,0:T(8,128)(2,1)}, bf16[128,2048]{1,0:T(8,128)(2,1)S(1)}, u32[]{:S(2)}) copy-start(bf16[128,2048]{1,0:T(8,128)(2,1)S(1)} %get-tuple-element.849) | copy-start | bytes 1572868
  239.7 3.9 %copy-start.24 = (bf16[128,2048]{1,0:T(8,128)(2,1)}, bf16[128,2048]{1,0:T(8,128)(2,1)S(1)}, u32[]{:S(2)}) copy-start(bf16[128,2048]{1,0:T(8,128)(2,1)S(1)} %get-tuple-element.848) | copy-start | bytes 1572868
  239.7 3.9 %copy-start.26 = (bf16[128,2048]{1,0:T(8,128)(2,1)}, bf16[128,2048]{1,0:T(8,128)(2,1)S(1)}, u32[]{:S(2)}) copy-start(bf16[128,2048]{1,0:T(8,128)(2,1)S(1)} %get-tuple-element.847) | copy-start | bytes 1572868
  239.8 2.6 copy-start.36
  242.4 2.2 copy-start.34
  244.6 4.1 %copy-start.31 = (bf16[384,1024]{1,0:T(8,128)(2,1)S(1)}, bf16[384,1024]{1,0:T(8,128)(2,1)}, u32[]{:S(2)}) copy-start(bf16[384,1024]{1,0:T(8,128)(2,1)} %multiply_convert_fusion) | copy-start | bytes 2359300
  250.4 10.1 %copy-start.27 = (bf16[128,2048]{1,0:T(8,128)(2,1)S(1)}, bf16[128,2048]{1,0:T(8,128)(2,1)}, u32[]{:S(2)}) copy-start(bf16[128,2048]{1,0:T(8,128)(2,1)} %copy-done.26) | copy-start | bytes 1572868
  250.4 10.1 %copy-start.25 = (bf16[128,2048]{1,0:T(8,128)(2,1)S(1)}, bf16[128,2048]{1,0:T(8,128)(2,1)}, u32[]{:S(2)}) copy-start(bf16[128,2048]{1,0:T(8,128)(2,1)} %copy-done.24) | copy-start | bytes 1572868
  250.4 11.6 %copy-start.23 = (bf16[128,2048]{1,0:T(8,128)(2,1)S(1)}, bf16[128,2048]{1,0:T(8,128)(2,1)}, u32[]{:S(2)}) copy-start(bf16[128,2048]{1,0:T(8,128)(2,1)} %copy-done.22) | copy-start | bytes 1572868
  250.4 44.8 %all-to-all-start.3 = ((bf16[16,24,1536]{2,1,0:T(8,128)(2,1)}), bf16[16,24,1536]{2,1,0:T(8,128)(2,1)}, u32[]{:S(2)}, u32[]{:S(2)}) async-start(bf16[16,24,1536]{2,1,0:T(8,128)(2,1)} %reorder.1), calls=%async_computation.3 | async-start | bytes 2359296 | tf_op jit(solution)/shard_map/all_to_all | solution.py:20
  257.5 6.0 %copy-start.48 = (f32[128]{0:T(128)S(1)}, f32[128]{0:T(128)}, u32[]{:S(2)}) copy-start(f32[128]{0:T(128)} %copy-done.47) | copy-start | bytes 1540
  257.6 6.4 %copy-start.46 = (f32[128]{0:T(128)S(1)}, f32[128]{0:T(128)}, u32[]{:S(2)}) copy-start(f32[128]{0:T(128)} %copy-done.45) | copy-start | bytes 1540
  259.9 19.9 %collective-permute-start.188 = (bf16[384,1024]{1,0:T(8,128)(2,1)}, bf16[384,1024]{1,0:T(8,128)(2,1)}, u32[]{:S(2)}, u32[]{:S(2)}) collective-permute-start(bf16[384,1024]{1,0:T(8,128)(2,1)} %broadcast_select_fusion.2), channel_id=1, source_target_pairs={{0,16},{16,0},{1,17},{17,1},{2,18},{18,2},{3,19},{19,3},{4,20},{20... | collective-permute-start | bytes 2359304 | tf_op jit(solution)/shard_map/ppermute | solution.py:57
  260.5 19.3 %copy-start.33 = (bf16[384,2048]{1,0:T(8,128)(2,1)S(1)}, bf16[384,2048]{1,0:T(8,128)(2,1)}, u32[]{:S(2)}) copy-start(bf16[384,2048]{1,0:T(8,128)(2,1)} %convolution_convert_fusion) | copy-start | bytes 4718596
  260.5 21.8 %collective-permute-start.189 = (bf16[128,2048]{1,0:T(8,128)(2,1)S(1)}, bf16[128,2048]{1,0:T(8,128)(2,1)S(1)}, u32[]{:S(2)}, u32[]{:S(2)}) collective-permute-start(bf16[128,2048]{1,0:T(8,128)(2,1)S(1)} %copy-done.27), channel_id=1, source_target_pairs={{0,1},{1,0},{2,3},{3,2},{4,5},{5,4},{6,7},{7,6},{8,9},{9,8},{10,11... | collective-permute-start | bytes 1572872 | tf_op jit(solution)/shard_map/ppermute | solution.py:249
  260.5 22.3 %collective-permute-start.190 = (bf16[128,2048]{1,0:T(8,128)(2,1)S(1)}, bf16[128,2048]{1,0:T(8,128)(2,1)S(1)}, u32[]{:S(2)}, u32[]{:S(2)}) collective-permute-start(bf16[128,2048]{1,0:T(8,128)(2,1)S(1)} %copy-done.25), channel_id=1, source_target_pairs={{0,2},{1,3},{2,0},{3,1},{4,6},{5,7},{6,4},{7,5},{8,10},{9,11},{10,... | collective-permute-start | bytes 1572872 | tf_op jit(solution)/shard_map/ppermute | solution.py:249
  262.1 33.2 %collective-permute-start.191 = (bf16[128,2048]{1,0:T(8,128)(2,1)S(1)}, bf16[128,2048]{1,0:T(8,128)(2,1)}, u32[]{:S(2)}, u32[]{:S(2)}) collective-permute-start(bf16[128,2048]{1,0:T(8,128)(2,1)S(1)} %copy-done.23), channel_id=1, source_target_pairs={{0,3},{1,2},{2,1},{3,0},{4,7},{5,6},{6,5},{7,4},{8,11},{9,10},{10,... | collective-permute-start | bytes 1572872 | tf_op jit(solution)/shard_map/ppermute | solution.py:249
  265.0 32.7 %copy-start.14 = (bf16[128,2048]{1,0:T(8,128)(2,1)S(1)}, bf16[128,2048]{1,0:T(8,128)(2,1)}, u32[]{:S(2)}) copy-start(bf16[128,2048]{1,0:T(8,128)(2,1)} %copy-done.13) | copy-start | bytes 1572868
  296.5 8.7 %copy-start.16 = (bf16[128,2048]{1,0:T(8,128)(2,1)S(1)}, bf16[128,2048]{1,0:T(8,128)(2,1)}, u32[]{:S(2)}) copy-start(bf16[128,2048]{1,0:T(8,128)(2,1)} %copy-done.15) | copy-start | bytes 1572868
  296.5 19.7 %collective-permute-start.192 = (bf16[384,1024]{1,0:T(8,128)(2,1)S(1)}, bf16[384,1024]{1,0:T(8,128)(2,1)}, u32[]{:S(2)}, u32[]{:S(2)}) collective-permute-start(bf16[384,1024]{1,0:T(8,128)(2,1)S(1)} %slice.87), channel_id=1, source_target_pairs={{0,16},{16,0},{1,17},{17,1},{2,18},{18,2},{3,19},{19,3},{4,20},{20... | collective-permute-start | bytes 2359304 | tf_op jit(solution)/shard_map/ppermute | solution.py:43
  300.6 23.7 %all-to-all-start.4 = ((bf16[16,24,1024]{2,1,0:T(8,128)(2,1)}), bf16[16,24,1024]{2,1,0:T(8,128)(2,1)S(1)}, u32[]{:S(2)}, u32[]{:S(2)}) async-start(bf16[16,24,1024]{2,1,0:T(8,128)(2,1)} %bitcast.22), calls=%async_computation.4 | async-start | bytes 1572864 | tf_op jit(solution)/shard_map/all_to_all | solution.py:20
  306.7 10.9 %copy-start.39 = (bf16[128,2048]{1,0:T(8,128)(2,1)S(1)}, bf16[128,2048]{1,0:T(8,128)(2,1)}, u32[]{:S(2)}) copy-start(bf16[128,2048]{1,0:T(8,128)(2,1)} %get-tuple-element.866) | copy-start | bytes 1572868
  306.8 10.9 %copy-start.40 = (bf16[128,2048]{1,0:T(8,128)(2,1)S(1)}, bf16[128,2048]{1,0:T(8,128)(2,1)}, u32[]{:S(2)}) copy-start(bf16[128,2048]{1,0:T(8,128)(2,1)} %get-tuple-element.867) | copy-start | bytes 1572868
  306.8 10.9 %copy-start.41 = (bf16[128,2048]{1,0:T(8,128)(2,1)S(1)}, bf16[128,2048]{1,0:T(8,128)(2,1)}, u32[]{:S(2)}) copy-start(bf16[128,2048]{1,0:T(8,128)(2,1)} %get-tuple-element.868) | copy-start | bytes 1572868
  306.8 10.9 %copy-start.42 = (bf16[128,2048]{1,0:T(8,128)(2,1)S(1)}, bf16[128,2048]{1,0:T(8,128)(2,1)}, u32[]{:S(2)}) copy-start(bf16[128,2048]{1,0:T(8,128)(2,1)} %get-tuple-element.869) | copy-start | bytes 1572868
  317.7 7.7 %copy-start.1 = (bf16[1,512,2048]{2,1,0:T(8,128)(2,1)S(1)}, bf16[1,512,2048]{2,1,0:T(8,128)(2,1)}, u32[]{:S(2)}) copy-start(bf16[1,512,2048]{2,1,0:T(8,128)(2,1)} %param.77) | copy-start | bytes 6291460
  (20 other events, 19.2 us)
